TPU v7x, 32 devices: a whole 2x2x4 slice. The times are simulated.
32 devices in a mesh: bz: 8 (over y, x, core), bxy: 4 (over z).
Axes of the slice: x: 2, y: 2, z: 4, core: 2. Of those that a mesh axis runs over, the one named last changes fastest.
Arguments:
- estimate: float32 [64, 64, 512], P('bz', 'bxy'), may hold values from 0.5 to 2
- observed: bfloat16 [3, 64, 64, 512], P(None, 'bz', 'bxy'), may hold values from 0.5 to 2
- psf_taps: float32 [3, 3, 3, 9], replicated, may hold values from 0.05 to 1
- view_shift: int32 [3], replicated, may hold values from 0 to 511
- intersection: int32 [3, 8, 4], replicated, may hold values 0 or 1
Outputs:
- updated: float32 [64, 64, 512], P('bz', 'bxy')
All inputs are finite; a program needn't handle non-finite values.
Results may differ from a plain program's by a relative error of at most 0.0004.
Values may be sent and summed in bfloat16 or wider, within the bound.
A program may use at most 64 MiB of HBM per device.

v0:
```python
import jax
import jax.numpy as jnp
from jax import lax
from jax.sharding import PartitionSpec as P

VIEWS = 3
RANK = 3
RADIUS = 4
PASSES = 8


EPS_TV = 0.25
TAU = 0.08
BACKGROUND = 0.1


def extended(cells, sides, width):
    for axis, dim in sides:
        count = lax.axis_size(axis)
        ends = count - 1
        head = lax.slice_in_dim(cells, 0, width, axis=dim)
        tail = lax.slice_in_dim(cells, cells.shape[dim] - width, cells.shape[dim], axis=dim)
        cells = jnp.concatenate(
            [
                lax.ppermute(tail, axis, [(i, (i + 1) % count) for i in range(ends)]),
                cells,
                lax.ppermute(head, axis, [((i + 1) % count, i) for i in range(ends)]),
            ],
            axis=dim,
        )
    return cells


def tv_pass(padded, z_first, x_first, cells_z, cells_x):
    rows_z = padded.shape[0] - 2
    rows_x = padded.shape[1] - 2
    field = padded[1:-1, 1:-1]
    zcoords = z_first + lax.iota(jnp.int32, rows_z + 2)
    xcoords = x_first + lax.iota(jnp.int32, rows_x + 2)
    z_inside = ((zcoords >= 0) & (zcoords < cells_z))[:, None, None]
    x_inside = ((xcoords >= 0) & (xcoords < cells_x))[None, :, None]
    y_lower = jnp.concatenate([field[:, :, :1], field[:, :, :-1]], axis=2)
    y_upper = jnp.concatenate([field[:, :, 1:], field[:, :, -1:]], axis=2)
    pairs = (
        (padded[:-2, 1:-1], z_inside[:-2]),
        (padded[2:, 1:-1], z_inside[2:]),
        (padded[1:-1, :-2], x_inside[:, :-2]),
        (padded[1:-1, 2:], x_inside[:, 2:]),
        (y_lower, True),
        (y_upper, True),
    )
    total = jnp.zeros_like(field)
    for beside, inside in pairs:
        diff = beside - field
        total = total + jnp.where(inside, diff / jnp.sqrt(diff * diff + EPS_TV), 0.0)
    return field + TAU * total


def conv_valid(values, kernel, axis):
    length = values.shape[axis] - (kernel.shape[0] - 1)
    total = kernel[0] * lax.slice_in_dim(values, 0, length, axis=axis)
    for tap in range(1, kernel.shape[0]):
        total = total + kernel[tap] * lax.slice_in_dim(values, tap, tap + length, axis=axis)
    return total


def conv_along_y(values, kernel):
    padded = jnp.pad(values, ((0, 0), (0, 0), (RADIUS, RADIUS)))
    return conv_valid(padded, kernel, 2)


def local(estimate, observed, psf_taps, view_shift, intersection):
    cz_here, cx_here, cells_y = estimate.shape
    bricks_z = lax.axis_size("bz")
    bricks_x = lax.axis_size("bxy")
    cells_z = cz_here * bricks_z
    cells_x = cx_here * bricks_x
    brick_z = lax.axis_index("bz")
    brick_x = lax.axis_index("bxy")
    z_base = brick_z * cz_here
    x_base = brick_x * cx_here
    smoothed = extended(estimate.astype(jnp.bfloat16), (("bz", 0), ("bxy", 1)), PASSES).astype(
        estimate.dtype
    )
    for pass_index in range(PASSES):
        smoothed = tv_pass(
            smoothed, z_base - PASSES + pass_index, x_base - PASSES + pass_index, cells_z, cells_x
        )
    sent = smoothed.astype(jnp.bfloat16)
    width = RADIUS
    sent_pad = extended(sent, (("bz", 0), ("bxy", 1)), width)
    sent_full = lax.optimization_barrier(sent_pad).astype(jnp.float32)
    kernels = psf_taps / jnp.sum(psf_taps, axis=-1, keepdims=True)
    images = []
    for view in range(VIEWS):
        moved = jnp.roll(sent_full, view_shift[view], axis=2)
        image = None
        for rank_index in range(RANK):
            blurred = conv_along_y(moved, kernels[view, rank_index, 2])
            blurred = conv_valid(blurred, kernels[view, rank_index, 1], 1)
            blurred = conv_valid(blurred, kernels[view, rank_index, 0], 0)
            image = blurred if image is None else image + blurred
        images.append(image / RANK)
    ratios = []
    for view in range(VIEWS):
        flag = intersection[view, brick_z, brick_x]
        ratio = jnp.where(
            flag > 0, observed[view].astype(jnp.float32) / (images[view] + BACKGROUND), 1.0
        )
        ratios.append(ratio.astype(jnp.bfloat16))
    ratio_pad = extended(jnp.stack(ratios, axis=0), (("bz", 1), ("bxy", 2)), RADIUS)
    ratio_full = lax.optimization_barrier(ratio_pad).astype(jnp.float32)
    correction = jnp.zeros(estimate.shape, jnp.float32)
    for view in range(VIEWS):
        back = None
        for rank_index in range(RANK):
            spread = conv_valid(ratio_full[view], kernels[view, rank_index, 0][::-1], 0)
            spread = conv_valid(spread, kernels[view, rank_index, 1][::-1], 1)
            spread = conv_along_y(spread, kernels[view, rank_index, 2][::-1])
            back = spread if back is None else back + spread
        back = back / RANK
        correction = correction + jnp.roll(back, -view_shift[view], axis=2)
    return smoothed * correction / VIEWS


def solution(mesh):
    return jax.shard_map(
        local,
        mesh=mesh,
        in_specs=(P("bz", "bxy", None), P(None, "bz", "bxy", None), P(), P(), P()),
        out_specs=P("bz", "bxy", None),
        check_vma=False,
    )
```

profile of v0, /device:TPU:3, one launch (start us, length us, event | category | flops | bytes accessed | tf_op | source)
XLA Modules:
  0.0 434.8 jit_solution(17618624749562967142)
XLA Ops:
  1.0 3.7 collective-permute-start
  4.7 1.9 collective-permute-start.1
  16.8 1.4 fusion.436
  24.6 1.4 constant_dynamic-slice_fusion
  28.6 3.2 collective-permute-start.2
  33.2 2.2 collective-permute-done.2
  35.4 3.8 collective-permute-done.3
  40.3 3.1 multiply_add_fusion
  44.2 2.5 multiply_add_fusion.1
  47.4 2.3 multiply_add_fusion.2
  56.6 5.0 %collective-permute-start.4 = (bf16[4,16,512]{2,1,0:T(8,128)(2,1)S(1)}, bf16[4,16,512]{2,1,0:T(8,128)(2,1)S(1)}, u32[]{:S(2)}, u32[]{:S(2)}) collective-permute-start(bf16[4,16,512]{2,1,0:T(8,128)(2,1)S(1)} %get-tuple-element.52), channel_id=1, source_target_pairs={{0,4},{4,8},{8,12},{12,16},{16,20},{20,24},{24,28},{1,5},{5,9},{9,... | collective-permute-start | bytes 196616 | tf_op jit(solution)/shard_map/ppermute | solution.py:25
  61.6 1.9 collective-permute-start.5
  64.3 3.8 collective-permute-done.5
  68.1 3.2 collective-permute-start.6
  71.3 1.7 collective-permute-start.7
  73.8 2.6 collective-permute-done.7
  77.9 7.2 %multiply_add_fusion.9 = f32[16,24,512]{2,1,0:T(8,128)S(1)} fusion(f32[16,24,512]{2,1,0:T(8,128)S(1)} %get-tuple-element.27, f32[]{:T(128)} %bitcast.83, f32[]{:T(128)} %bitcast.82, f32[]{:T(128)} %bitcast.81, f32[]{:T(128)} %bitcast.80, f32[]{:T(128)} %bitcast.79, f32[]{:T(128)} %bitcast.78, f32[]{:T(128)} %bitcast.77, f32[]{:T(128)} %bitcast.76, f32[]{:T(128)} %bitcast.75), kind=kLoop, calls=%fused_computation.68 | loop fusion | flops 3342336 | bytes 1572900 | tf_op jit(solution)/shard_map/add | solution.py:63
  85.2 7.4 %multiply_add_fusion.10 = f32[16,24,512]{2,1,0:T(8,128)S(1)} fusion(f32[16,24,512]{2,1,0:T(8,128)S(1)} %get-tuple-element.27, f32[]{:T(128)} %bitcast.56, f32[]{:T(128)} %bitcast.55, f32[]{:T(128)} %bitcast.54, f32[]{:T(128)} %bitcast.53, f32[]{:T(128)} %bitcast.52, f32[]{:T(128)} %bitcast.51, f32[]{:T(128)} %bitcast.50, f32[]{:T(128)} %bitcast.49, f32[]{:T(128)} %bitcast.48), kind=kLoop, calls=%fused_computation.69 | loop fusion | flops 3342336 | bytes 1572900 | tf_op jit(solution)/shard_map/add | solution.py:63
  92.5 7.2 %multiply_add_fusion.11 = f32[16,24,512]{2,1,0:T(8,128)S(1)} fusion(f32[16,24,512]{2,1,0:T(8,128)S(1)} %get-tuple-element.27, f32[]{:T(128)} %bitcast.16, f32[]{:T(128)} %bitcast.31, f32[]{:T(128)} %bitcast.30, f32[]{:T(128)} %bitcast.29, f32[]{:T(128)} %bitcast.28, f32[]{:T(128)} %bitcast.27, f32[]{:T(128)} %bitcast.26, f32[]{:T(128)} %bitcast.25, f32[]{:T(128)} %bitcast.23), kind=kLoop, calls=%fused_computation.70 | loop fusion | flops 3342336 | bytes 1572900 | tf_op jit(solution)/shard_map/add | solution.py:63
  99.7 7.4 %multiply_add_fusion.6 = f32[16,24,512]{2,1,0:T(8,128)S(1)} fusion(f32[16,24,512]{2,1,0:T(8,128)S(1)} %get-tuple-element.28, f32[]{:T(128)} %bitcast.168, f32[]{:T(128)} %bitcast.167, f32[]{:T(128)} %bitcast.166, f32[]{:T(128)} %bitcast.165, f32[]{:T(128)} %bitcast.164, f32[]{:T(128)} %bitcast.163, f32[]{:T(128)} %bitcast.162, f32[]{:T(128)} %bitcast.161, ...), kind=kLoop, calls=%fused_computation.65 | loop fusion | flops 3342336 | bytes 1572900 | tf_op jit(solution)/shard_map/add | solution.py:63
  107.1 7.2 %multiply_add_fusion.7 = f32[16,24,512]{2,1,0:T(8,128)S(1)} fusion(f32[16,24,512]{2,1,0:T(8,128)S(1)} %get-tuple-element.28, f32[]{:T(128)} %bitcast.141, f32[]{:T(128)} %bitcast.140, f32[]{:T(128)} %bitcast.139, f32[]{:T(128)} %bitcast.138, f32[]{:T(128)} %bitcast.137, f32[]{:T(128)} %bitcast.136, f32[]{:T(128)} %bitcast.135, f32[]{:T(128)} %bitcast.134, ...), kind=kLoop, calls=%fused_computation.66 | loop fusion | flops 3342336 | bytes 1572900 | tf_op jit(solution)/shard_map/add | solution.py:63
  114.4 7.1 %multiply_add_fusion.8 = f32[16,24,512]{2,1,0:T(8,128)S(1)} fusion(f32[16,24,512]{2,1,0:T(8,128)S(1)} %get-tuple-element.28, f32[]{:T(128)} %bitcast.114, f32[]{:T(128)} %bitcast.113, f32[]{:T(128)} %bitcast.112, f32[]{:T(128)} %bitcast.111, f32[]{:T(128)} %bitcast.110, f32[]{:T(128)} %bitcast.109, f32[]{:T(128)} %bitcast.108, f32[]{:T(128)} %bitcast.107, ...), kind=kLoop, calls=%fused_computation.67 | loop fusion | flops 3342336 | bytes 1572900 | tf_op jit(solution)/shard_map/add | solution.py:63
  121.5 7.4 %multiply_add_fusion.4 = f32[16,24,512]{2,1,0:T(8,128)S(1)} fusion(f32[16,24,512]{2,1,0:T(8,128)S(1)} %get-tuple-element.29, f32[]{:T(128)} %bitcast.226, f32[]{:T(128)} %bitcast.225, f32[]{:T(128)} %bitcast.224, f32[]{:T(128)} %bitcast.223, f32[]{:T(128)} %bitcast.222, f32[]{:T(128)} %bitcast.221, f32[]{:T(128)} %bitcast.220, f32[]{:T(128)} %bitcast.219, ...), kind=kLoop, calls=%fused_computation.63 | loop fusion | flops 3342336 | bytes 1572900 | tf_op jit(solution)/shard_map/add | solution.py:63
  128.9 7.3 %multiply_add_fusion.5 = f32[16,24,512]{2,1,0:T(8,128)S(1)} fusion(f32[16,24,512]{2,1,0:T(8,128)S(1)} %get-tuple-element.29, f32[]{:T(128)} %bitcast.199, f32[]{:T(128)} %bitcast.198, f32[]{:T(128)} %bitcast.197, f32[]{:T(128)} %bitcast.196, f32[]{:T(128)} %bitcast.195, f32[]{:T(128)} %bitcast.194, f32[]{:T(128)} %bitcast.193, f32[]{:T(128)} %bitcast.192, ...), kind=kLoop, calls=%fused_computation.64 | loop fusion | flops 3342336 | bytes 1572900 | tf_op jit(solution)/shard_map/add | solution.py:63
  136.2 7.3 %multiply_add_fusion.3 = f32[16,24,512]{2,1,0:T(8,128)S(1)} fusion(f32[16,24,512]{2,1,0:T(8,128)S(1)} %get-tuple-element.29, f32[]{:T(128)} %bitcast.253, f32[]{:T(128)} %bitcast.252, f32[]{:T(128)} %bitcast.251, f32[]{:T(128)} %bitcast.250, f32[]{:T(128)} %bitcast.249, f32[]{:T(128)} %bitcast.248, f32[]{:T(128)} %bitcast.247, f32[]{:T(128)} %bitcast.246, ...), kind=kLoop, calls=%fused_computation.62 | loop fusion | flops 3342336 | bytes 1572900 | tf_op jit(solution)/shard_map/add | solution.py:63
  143.6 6.2 %fusion.51 = f32[16,16,512]{2,1,0:T(8,128)S(1)} fusion(f32[16,24,512]{2,1,0:T(8,128)S(1)} %multiply_add_fusion.9, f32[]{:T(128)} %bitcast.91, f32[]{:T(128)} %bitcast.90, f32[]{:T(128)} %bitcast.89, f32[]{:T(128)} %bitcast.88, f32[]{:T(128)} %bitcast.87, f32[]{:T(128)} %bitcast.86, f32[]{:T(128)} %bitcast.85, f32[]{:T(128)} %bitcast.84, f32[]{:T(128)} %bitcast.74), kind=kLoop, calls=%fused_computation.189 | loop fusion | flops 2228224 | bytes 5242916 | tf_op jit(solution)/shard_map/add | solution.py:63
  149.8 6.2 %fusion.59 = f32[16,16,512]{2,1,0:T(8,128)S(1)} fusion(f32[16,24,512]{2,1,0:T(8,128)S(1)} %multiply_add_fusion.10, f32[]{:T(128)} %bitcast.64, f32[]{:T(128)} %bitcast.63, f32[]{:T(128)} %bitcast.62, f32[]{:T(128)} %bitcast.61, f32[]{:T(128)} %bitcast.60, f32[]{:T(128)} %bitcast.59, f32[]{:T(128)} %bitcast.58, f32[]{:T(128)} %bitcast.57, f32[]{:T(128)} %bitcast.47), kind=kLoop, calls=%fused_computation.206 | loop fusion | flops 2228224 | bytes 5242916 | tf_op jit(solution)/shard_map/add | solution.py:63
  156.0 6.1 %fusion.67 = f32[16,16,512]{2,1,0:T(8,128)S(1)} fusion(f32[16,24,512]{2,1,0:T(8,128)S(1)} %multiply_add_fusion.11, f32[]{:T(128)} %bitcast.17, f32[]{:T(128)} %bitcast.38, f32[]{:T(128)} %bitcast.37, f32[]{:T(128)} %bitcast.36, f32[]{:T(128)} %bitcast.35, f32[]{:T(128)} %bitcast.34, f32[]{:T(128)} %bitcast.33, f32[]{:T(128)} %bitcast.32, f32[]{:T(128)} %bitcast.22), kind=kLoop, calls=%fused_computation.223 | loop fusion | flops 2228224 | bytes 5242916 | tf_op jit(solution)/shard_map/add | solution.py:63
  162.1 5.9 %fusion.27 = f32[16,16,512]{2,1,0:T(8,128)S(1)} fusion(f32[16,24,512]{2,1,0:T(8,128)S(1)} %multiply_add_fusion.6, f32[]{:T(128)} %bitcast.176, f32[]{:T(128)} %bitcast.175, f32[]{:T(128)} %bitcast.174, f32[]{:T(128)} %bitcast.173, f32[]{:T(128)} %bitcast.172, f32[]{:T(128)} %bitcast.171, f32[]{:T(128)} %bitcast.170, f32[]{:T(128)} %bitcast.169, f32[]{:T(128)} %bitcast.159), kind=kLoop, calls=%fused_computation.138 | loop fusion | flops 2228224 | bytes 5242916 | tf_op jit(solution)/shard_map/add | solution.py:63
  168.1 5.9 %fusion.35 = f32[16,16,512]{2,1,0:T(8,128)S(1)} fusion(f32[16,24,512]{2,1,0:T(8,128)S(1)} %multiply_add_fusion.7, f32[]{:T(128)} %bitcast.149, f32[]{:T(128)} %bitcast.148, f32[]{:T(128)} %bitcast.147, f32[]{:T(128)} %bitcast.146, f32[]{:T(128)} %bitcast.145, f32[]{:T(128)} %bitcast.144, f32[]{:T(128)} %bitcast.143, f32[]{:T(128)} %bitcast.142, f32[]{:T(128)} %bitcast.132), kind=kLoop, calls=%fused_computation.155 | loop fusion | flops 2228224 | bytes 5242916 | tf_op jit(solution)/shard_map/add | solution.py:63
  174.0 6.3 %fusion.43 = f32[16,16,512]{2,1,0:T(8,128)S(1)} fusion(f32[16,24,512]{2,1,0:T(8,128)S(1)} %multiply_add_fusion.8, f32[]{:T(128)} %bitcast.122, f32[]{:T(128)} %bitcast.121, f32[]{:T(128)} %bitcast.120, f32[]{:T(128)} %bitcast.119, f32[]{:T(128)} %bitcast.118, f32[]{:T(128)} %bitcast.117, f32[]{:T(128)} %bitcast.116, f32[]{:T(128)} %bitcast.115, f32[]{:T(128)} %bitcast.104), kind=kLoop, calls=%fused_computation.172 | loop fusion | flops 2228224 | bytes 5242916 | tf_op jit(solution)/shard_map/add | solution.py:63
  180.3 6.1 %fusion.11 = f32[16,16,512]{2,1,0:T(8,128)S(1)} fusion(f32[16,24,512]{2,1,0:T(8,128)S(1)} %multiply_add_fusion.4, f32[]{:T(128)} %bitcast.234, f32[]{:T(128)} %bitcast.233, f32[]{:T(128)} %bitcast.232, f32[]{:T(128)} %bitcast.231, f32[]{:T(128)} %bitcast.230, f32[]{:T(128)} %bitcast.229, f32[]{:T(128)} %bitcast.228, f32[]{:T(128)} %bitcast.227, f32[]{:T(128)} %bitcast.217), kind=kLoop, calls=%fused_computation.104 | loop fusion | flops 2228224 | bytes 5242916 | tf_op jit(solution)/shard_map/add | solution.py:63
  186.3 6.2 %fusion.19 = f32[16,16,512]{2,1,0:T(8,128)S(1)} fusion(f32[16,24,512]{2,1,0:T(8,128)S(1)} %multiply_add_fusion.5, f32[]{:T(128)} %bitcast.207, f32[]{:T(128)} %bitcast.206, f32[]{:T(128)} %bitcast.205, f32[]{:T(128)} %bitcast.204, f32[]{:T(128)} %bitcast.203, f32[]{:T(128)} %bitcast.202, f32[]{:T(128)} %bitcast.201, f32[]{:T(128)} %bitcast.200, f32[]{:T(128)} %bitcast.189), kind=kLoop, calls=%fused_computation.121 | loop fusion | flops 2228224 | bytes 5242916 | tf_op jit(solution)/shard_map/add | solution.py:63
  192.5 6.3 %fusion.3 = f32[16,16,512]{2,1,0:T(8,128)S(1)} fusion(f32[16,24,512]{2,1,0:T(8,128)S(1)} %multiply_add_fusion.3, f32[]{:T(128)} %bitcast.261, f32[]{:T(128)} %bitcast.260, f32[]{:T(128)} %bitcast.259, f32[]{:T(128)} %bitcast.258, f32[]{:T(128)} %bitcast.257, f32[]{:T(128)} %bitcast.256, f32[]{:T(128)} %bitcast.255, f32[]{:T(128)} %bitcast.254, f32[]{:T(128)} %bitcast.244), kind=kLoop, calls=%fused_computation.87 | loop fusion | flops 2228224 | bytes 5242916 | tf_op jit(solution)/shard_map/add | solution.py:63
  198.8 17.3 %fusion.402 = bf16[1,8,16,512]{3,2,1,0:T(8,128)(2,1)S(1)} fusion(f32[16,16,512]{2,1,0:T(8,128)S(1)} %fusion.51, f32[]{:T(128)} %bitcast.99, f32[]{:T(128)} %bitcast.98, f32[]{:T(128)} %bitcast.97, f32[]{:T(128)} %bitcast.96, f32[]{:T(128)} %bitcast.95, f32[]{:T(128)} %bitcast.94, f32[]{:T(128)} %bitcast.93, f32[]{:T(128)} %bitcast.92, f32[]{:T(128)} %bitcast.73, ...), kind=kLoop, calls=%fused_computation.837 | loop fusion | flops 3866624 | bytes 7340141 | tf_op jit(solution)/shard_map/stack | solution.py:111
  216.2 17.2 %fusion.401 = bf16[1,8,16,512]{3,2,1,0:T(8,128)(2,1)S(1)} fusion(f32[16,16,512]{2,1,0:T(8,128)S(1)} %fusion.27, f32[]{:T(128)} %bitcast.184, f32[]{:T(128)} %bitcast.183, f32[]{:T(128)} %bitcast.182, f32[]{:T(128)} %bitcast.181, f32[]{:T(128)} %bitcast.180, f32[]{:T(128)} %bitcast.179, f32[]{:T(128)} %bitcast.178, f32[]{:T(128)} %bitcast.177, f32[]{:T(128)} %bitcast.158, ...), kind=kLoop, calls=%fused_computation.836 | loop fusion | flops 3866624 | bytes 7340141 | tf_op jit(solution)/shard_map/stack | solution.py:111
  233.4 17.3 %fusion.400 = bf16[1,8,16,512]{3,2,1,0:T(8,128)(2,1)S(1)} fusion(f32[16,16,512]{2,1,0:T(8,128)S(1)} %fusion.3, f32[]{:T(128)} %bitcast.269, f32[]{:T(128)} %bitcast.268, f32[]{:T(128)} %bitcast.267, f32[]{:T(128)} %bitcast.266, f32[]{:T(128)} %bitcast.265, f32[]{:T(128)} %bitcast.264, f32[]{:T(128)} %bitcast.263, f32[]{:T(128)} %bitcast.262, f32[]{:T(128)} %bitcast.243, ...), kind=kLoop, calls=%fused_computation.835 | loop fusion | flops 3866624 | bytes 7340141 | tf_op jit(solution)/shard_map/stack | solution.py:111
  250.7 3.3 collective-permute-start.8
  254.0 1.9 collective-permute-start.9
  257.0 4.9 %collective-permute-done.9 = bf16[3,4,16,512]{3,2,1,0:T(8,128)(2,1)S(1)} collective-permute-done((bf16[3,4,16,512]{3,2,1,0:T(8,128)(2,1)S(1)}, bf16[3,4,16,512]{3,2,1,0:T(8,128)(2,1)S(1)}, u32[]{:S(2)}, u32[]{:S(2)}) %collective-permute-start.9) | collective-permute-done | bytes 196640 | tf_op jit(solution)/shard_map/ppermute | solution.py:27
  262.1 3.2 collective-permute-start.10
  265.3 1.5 collective-permute-start.11
  268.8 3.0 collective-permute-done.11
  272.9 5.7 %add_bitcast_fusion.6 = f32[8,24,512]{2,1,0:T(8,128)S(1)} fusion(f32[3,16,24,512]{3,2,1,0:T(8,128)S(1)} %convert_element_type.75, f32[]{:T(128)} %bitcast.73, f32[]{:T(128)} %bitcast.92, f32[]{:T(128)} %bitcast.93, f32[]{:T(128)} %bitcast.94, f32[]{:T(128)} %bitcast.95, f32[]{:T(128)} %bitcast.96, f32[]{:T(128)} %bitcast.97, f32[]{:T(128)} %bitcast.98, ...), kind=kLoop, calls=%fused_computation.333 | loop fusion | flops 1671168 | bytes 3932196 | tf_op jit(solution)/shard_map/add | solution.py:63
  278.5 5.8 %add_bitcast_fusion.7 = f32[8,24,512]{2,1,0:T(8,128)S(1)} fusion(f32[3,16,24,512]{3,2,1,0:T(8,128)S(1)} %convert_element_type.75, f32[]{:T(128)} %bitcast.46, f32[]{:T(128)} %bitcast.65, f32[]{:T(128)} %bitcast.66, f32[]{:T(128)} %bitcast.67, f32[]{:T(128)} %bitcast.68, f32[]{:T(128)} %bitcast.69, f32[]{:T(128)} %bitcast.70, f32[]{:T(128)} %bitcast.71, ...), kind=kLoop, calls=%fused_computation.334 | loop fusion | flops 1671168 | bytes 3932196 | tf_op jit(solution)/shard_map/add | solution.py:63
  284.3 6.0 %add_bitcast_fusion.8 = f32[8,24,512]{2,1,0:T(8,128)S(1)} fusion(f32[3,16,24,512]{3,2,1,0:T(8,128)S(1)} %convert_element_type.75, f32[]{:T(128)} %bitcast.21, f32[]{:T(128)} %bitcast.39, f32[]{:T(128)} %bitcast.40, f32[]{:T(128)} %bitcast.41, f32[]{:T(128)} %bitcast.42, f32[]{:T(128)} %bitcast.43, f32[]{:T(128)} %bitcast.44, f32[]{:T(128)} %bitcast.45, ...), kind=kLoop, calls=%fused_computation.335 | loop fusion | flops 1671168 | bytes 3932196 | tf_op jit(solution)/shard_map/add | solution.py:63
  290.4 5.9 %add_bitcast_fusion.3 = f32[8,24,512]{2,1,0:T(8,128)S(1)} fusion(f32[3,16,24,512]{3,2,1,0:T(8,128)S(1)} %convert_element_type.75, f32[]{:T(128)} %bitcast.158, f32[]{:T(128)} %bitcast.177, f32[]{:T(128)} %bitcast.178, f32[]{:T(128)} %bitcast.179, f32[]{:T(128)} %bitcast.180, f32[]{:T(128)} %bitcast.181, f32[]{:T(128)} %bitcast.182, f32[]{:T(128)} %bitcast.183, ...), kind=kLoop, calls=%fused_computation.330 | loop fusion | flops 1671168 | bytes 3932196 | tf_op jit(solution)/shard_map/add | solution.py:63
  296.3 5.7 %add_bitcast_fusion.5 = f32[8,24,512]{2,1,0:T(8,128)S(1)} fusion(f32[3,16,24,512]{3,2,1,0:T(8,128)S(1)} %convert_element_type.75, f32[]{:T(128)} %bitcast.103, f32[]{:T(128)} %bitcast.123, f32[]{:T(128)} %bitcast.124, f32[]{:T(128)} %bitcast.125, f32[]{:T(128)} %bitcast.126, f32[]{:T(128)} %bitcast.127, f32[]{:T(128)} %bitcast.128, f32[]{:T(128)} %bitcast.129, ...), kind=kLoop, calls=%fused_computation.332 | loop fusion | flops 1671168 | bytes 3932196 | tf_op jit(solution)/shard_map/add | solution.py:63
  302.0 5.7 %add_bitcast_fusion.4 = f32[8,24,512]{2,1,0:T(8,128)S(1)} fusion(f32[3,16,24,512]{3,2,1,0:T(8,128)S(1)} %convert_element_type.75, f32[]{:T(128)} %bitcast.131, f32[]{:T(128)} %bitcast.150, f32[]{:T(128)} %bitcast.151, f32[]{:T(128)} %bitcast.152, f32[]{:T(128)} %bitcast.153, f32[]{:T(128)} %bitcast.154, f32[]{:T(128)} %bitcast.155, f32[]{:T(128)} %bitcast.156, ...), kind=kLoop, calls=%fused_computation.331 | loop fusion | flops 1671168 | bytes 3932196 | tf_op jit(solution)/shard_map/add | solution.py:63
  307.7 5.8 %add_bitcast_fusion = f32[8,24,512]{2,1,0:T(8,128)S(1)} fusion(f32[3,16,24,512]{3,2,1,0:T(8,128)S(1)} %convert_element_type.75, f32[]{:T(128)} %bitcast.243, f32[]{:T(128)} %bitcast.262, f32[]{:T(128)} %bitcast.263, f32[]{:T(128)} %bitcast.264, f32[]{:T(128)} %bitcast.265, f32[]{:T(128)} %bitcast.266, f32[]{:T(128)} %bitcast.267, f32[]{:T(128)} %bitcast.268, ...), kind=kLoop, calls=%fused_computation.327 | loop fusion | flops 1671168 | bytes 3932196 | tf_op jit(solution)/shard_map/add | solution.py:63
  313.6 5.7 %add_bitcast_fusion.1 = f32[8,24,512]{2,1,0:T(8,128)S(1)} fusion(f32[3,16,24,512]{3,2,1,0:T(8,128)S(1)} %convert_element_type.75, f32[]{:T(128)} %bitcast.216, f32[]{:T(128)} %bitcast.235, f32[]{:T(128)} %bitcast.236, f32[]{:T(128)} %bitcast.237, f32[]{:T(128)} %bitcast.238, f32[]{:T(128)} %bitcast.239, f32[]{:T(128)} %bitcast.240, f32[]{:T(128)} %bitcast.241, ...), kind=kLoop, calls=%fused_computation.328 | loop fusion | flops 1671168 | bytes 3932196 | tf_op jit(solution)/shard_map/add | solution.py:63
  319.3 5.9 %add_bitcast_fusion.2 = f32[8,24,512]{2,1,0:T(8,128)S(1)} fusion(f32[3,16,24,512]{3,2,1,0:T(8,128)S(1)} %convert_element_type.75, f32[]{:T(128)} %bitcast.188, f32[]{:T(128)} %bitcast.208, f32[]{:T(128)} %bitcast.209, f32[]{:T(128)} %bitcast.210, f32[]{:T(128)} %bitcast.211, f32[]{:T(128)} %bitcast.212, f32[]{:T(128)} %bitcast.213, f32[]{:T(128)} %bitcast.214, ...), kind=kLoop, calls=%fused_computation.329 | loop fusion | flops 1671168 | bytes 3932196 | tf_op jit(solution)/shard_map/add | solution.py:63
  325.1 5.9 %fusion.283 = f32[8,16,512]{2,1,0:T(8,128)S(1)} fusion(f32[8,24,512]{2,1,0:T(8,128)S(1)} %add_bitcast_fusion.6, f32[]{:T(128)} %bitcast.74, f32[]{:T(128)} %bitcast.84, f32[]{:T(128)} %bitcast.85, f32[]{:T(128)} %bitcast.86, f32[]{:T(128)} %bitcast.87, f32[]{:T(128)} %bitcast.88, f32[]{:T(128)} %bitcast.89, f32[]{:T(128)} %bitcast.90, f32[]{:T(128)} %bitcast.91), kind=kLoop, calls=%fused_computation.599 | loop fusion | flops 1114112 | bytes 2621476 | tf_op jit(solution)/shard_map/add | solution.py:63
  331.1 6.0 %fusion.291 = f32[8,16,512]{2,1,0:T(8,128)S(1)} fusion(f32[8,24,512]{2,1,0:T(8,128)S(1)} %add_bitcast_fusion.7, f32[]{:T(128)} %bitcast.47, f32[]{:T(128)} %bitcast.57, f32[]{:T(128)} %bitcast.58, f32[]{:T(128)} %bitcast.59, f32[]{:T(128)} %bitcast.60, f32[]{:T(128)} %bitcast.61, f32[]{:T(128)} %bitcast.62, f32[]{:T(128)} %bitcast.63, f32[]{:T(128)} %bitcast.64), kind=kLoop, calls=%fused_computation.616 | loop fusion | flops 1114112 | bytes 2621476 | tf_op jit(solution)/shard_map/add | solution.py:63
  337.1 5.8 %fusion.299 = f32[8,16,512]{2,1,0:T(8,128)S(1)} fusion(f32[8,24,512]{2,1,0:T(8,128)S(1)} %add_bitcast_fusion.8, f32[]{:T(128)} %bitcast.22, f32[]{:T(128)} %bitcast.32, f32[]{:T(128)} %bitcast.33, f32[]{:T(128)} %bitcast.34, f32[]{:T(128)} %bitcast.35, f32[]{:T(128)} %bitcast.36, f32[]{:T(128)} %bitcast.37, f32[]{:T(128)} %bitcast.38, f32[]{:T(128)} %bitcast.17), kind=kLoop, calls=%fused_computation.633 | loop fusion | flops 1114112 | bytes 2621476 | tf_op jit(solution)/shard_map/add | solution.py:63
  342.9 5.7 %fusion.259 = f32[8,16,512]{2,1,0:T(8,128)S(1)} fusion(f32[8,24,512]{2,1,0:T(8,128)S(1)} %add_bitcast_fusion.3, f32[]{:T(128)} %bitcast.159, f32[]{:T(128)} %bitcast.169, f32[]{:T(128)} %bitcast.170, f32[]{:T(128)} %bitcast.171, f32[]{:T(128)} %bitcast.172, f32[]{:T(128)} %bitcast.173, f32[]{:T(128)} %bitcast.174, f32[]{:T(128)} %bitcast.175, f32[]{:T(128)} %bitcast.176), kind=kLoop, calls=%fused_computation.548 | loop fusion | flops 1114112 | bytes 2621476 | tf_op jit(solution)/shard_map/add | solution.py:63
  348.6 6.0 %fusion.275 = f32[8,16,512]{2,1,0:T(8,128)S(1)} fusion(f32[8,24,512]{2,1,0:T(8,128)S(1)} %add_bitcast_fusion.5, f32[]{:T(128)} %bitcast.104, f32[]{:T(128)} %bitcast.115, f32[]{:T(128)} %bitcast.116, f32[]{:T(128)} %bitcast.117, f32[]{:T(128)} %bitcast.118, f32[]{:T(128)} %bitcast.119, f32[]{:T(128)} %bitcast.120, f32[]{:T(128)} %bitcast.121, f32[]{:T(128)} %bitcast.122), kind=kLoop, calls=%fused_computation.582 | loop fusion | flops 1114112 | bytes 2621476 | tf_op jit(solution)/shard_map/add | solution.py:63
  354.6 5.7 %fusion.267 = f32[8,16,512]{2,1,0:T(8,128)S(1)} fusion(f32[8,24,512]{2,1,0:T(8,128)S(1)} %add_bitcast_fusion.4, f32[]{:T(128)} %bitcast.132, f32[]{:T(128)} %bitcast.142, f32[]{:T(128)} %bitcast.143, f32[]{:T(128)} %bitcast.144, f32[]{:T(128)} %bitcast.145, f32[]{:T(128)} %bitcast.146, f32[]{:T(128)} %bitcast.147, f32[]{:T(128)} %bitcast.148, f32[]{:T(128)} %bitcast.149), kind=kLoop, calls=%fused_computation.565 | loop fusion | flops 1114112 | bytes 2621476 | tf_op jit(solution)/shard_map/add | solution.py:63
  360.3 6.0 %fusion.235 = f32[8,16,512]{2,1,0:T(8,128)S(1)} fusion(f32[8,24,512]{2,1,0:T(8,128)S(1)} %add_bitcast_fusion, f32[]{:T(128)} %bitcast.244, f32[]{:T(128)} %bitcast.254, f32[]{:T(128)} %bitcast.255, f32[]{:T(128)} %bitcast.256, f32[]{:T(128)} %bitcast.257, f32[]{:T(128)} %bitcast.258, f32[]{:T(128)} %bitcast.259, f32[]{:T(128)} %bitcast.260, f32[]{:T(128)} %bitcast.261), kind=kLoop, calls=%fused_computation.497 | loop fusion | flops 1114112 | bytes 2621476 | tf_op jit(solution)/shard_map/add | solution.py:63
  366.2 5.8 %fusion.243 = f32[8,16,512]{2,1,0:T(8,128)S(1)} fusion(f32[8,24,512]{2,1,0:T(8,128)S(1)} %add_bitcast_fusion.1, f32[]{:T(128)} %bitcast.217, f32[]{:T(128)} %bitcast.227, f32[]{:T(128)} %bitcast.228, f32[]{:T(128)} %bitcast.229, f32[]{:T(128)} %bitcast.230, f32[]{:T(128)} %bitcast.231, f32[]{:T(128)} %bitcast.232, f32[]{:T(128)} %bitcast.233, f32[]{:T(128)} %bitcast.234), kind=kLoop, calls=%fused_computation.514 | loop fusion | flops 1114112 | bytes 2621476 | tf_op jit(solution)/shard_map/add | solution.py:63
  372.0 5.9 %fusion.251 = f32[8,16,512]{2,1,0:T(8,128)S(1)} fusion(f32[8,24,512]{2,1,0:T(8,128)S(1)} %add_bitcast_fusion.2, f32[]{:T(128)} %bitcast.189, f32[]{:T(128)} %bitcast.200, f32[]{:T(128)} %bitcast.201, f32[]{:T(128)} %bitcast.202, f32[]{:T(128)} %bitcast.203, f32[]{:T(128)} %bitcast.204, f32[]{:T(128)} %bitcast.205, f32[]{:T(128)} %bitcast.206, f32[]{:T(128)} %bitcast.207), kind=kLoop, calls=%fused_computation.531 | loop fusion | flops 1114112 | bytes 2621476 | tf_op jit(solution)/shard_map/add | solution.py:63
  378.0 18.4 %fusion.86 = f32[8,16,512]{2,1,0:T(8,128)S(1)} fusion(f32[8,16,512]{2,1,0:T(8,128)S(1)} %fusion.299, f32[8,16,512]{2,1,0:T(8,128)S(1)} %fusion.291, f32[8,16,512]{2,1,0:T(8,128)S(1)} %fusion.283, f32[]{:T(128)} %bitcast.75, f32[]{:T(128)} %bitcast.76, f32[]{:T(128)} %bitcast.77, f32[]{:T(128)} %bitcast.78, f32[]{:T(128)} %bitcast.79, f32[]{:T(128)} %bitcast.80, ...), kind=kLoop, calls=%fused_computation.347 | loop fusion | flops 3538944 | bytes 1048684 | tf_op jit(solution)/shard_map/div | solution.py:121
  396.4 18.4 %fusion.137 = f32[8,16,512]{2,1,0:T(8,128)S(1)} fusion(f32[8,16,512]{2,1,0:T(8,128)S(1)} %fusion.275, f32[8,16,512]{2,1,0:T(8,128)S(1)} %fusion.267, f32[8,16,512]{2,1,0:T(8,128)S(1)} %fusion.259, f32[]{:T(128)} %bitcast.160, f32[]{:T(128)} %bitcast.161, f32[]{:T(128)} %bitcast.162, f32[]{:T(128)} %bitcast.163, f32[]{:T(128)} %bitcast.164, f32[]{:T(128)} %bitcast.165, ...), kind=kLoop, calls=%fused_computation.398 | loop fusion | flops 3538944 | bytes 1048684 | tf_op jit(solution)/shard_map/div | solution.py:121
  414.8 18.6 %fusion.188 = f32[8,16,512]{2,1,0:T(8,128)S(1)} fusion(f32[8,16,512]{2,1,0:T(8,128)S(1)} %fusion.251, f32[8,16,512]{2,1,0:T(8,128)S(1)} %fusion.243, f32[8,16,512]{2,1,0:T(8,128)S(1)} %fusion.235, f32[]{:T(128)} %bitcast.245, f32[]{:T(128)} %bitcast.246, f32[]{:T(128)} %bitcast.247, f32[]{:T(128)} %bitcast.248, f32[]{:T(128)} %bitcast.249, f32[]{:T(128)} %bitcast.250, ...), kind=kLoop, calls=%fused_computation.449 | loop fusion | flops 3538944 | bytes 1048684 | tf_op jit(solution)/shard_map/div | solution.py:121
  (93 shorter events, 29.8 us)
Async XLA Ops:
  1.0 27.6 %collective-permute-start = (bf16[8,16,512]{2,1,0:T(8,128)(2,1)S(1)}, bf16[8,16,512]{2,1,0:T(8,128)(2,1)S(1)}, u32[]{:S(2)}, u32[]{:S(2)}) collective-permute-start(bf16[8,16,512]{2,1,0:T(8,128)(2,1)S(1)} %convert_element_type.62), channel_id=1, source_target_pairs={{0,4},{4,8},{8,12},{12,16},{16,20},{20,24},{24,28},{1,5},{5,9},{9,... | collective-permute-start | bytes 393224 | tf_op jit(solution)/shard_map/ppermute | solution.py:25
  4.7 23.9 %collective-permute-start.1 = (bf16[8,16,512]{2,1,0:T(8,128)(2,1)S(1)}, bf16[8,16,512]{2,1,0:T(8,128)(2,1)S(1)}, u32[]{:S(2)}, u32[]{:S(2)}) collective-permute-start(bf16[8,16,512]{2,1,0:T(8,128)(2,1)S(1)} %convert_element_type.62), channel_id=1, source_target_pairs={{4,0},{8,4},{12,8},{16,12},{20,16},{24,20},{28,24},{5,1},{9,5},{13... | collective-permute-start | bytes 393224 | tf_op jit(solution)/shard_map/ppermute | solution.py:27
  28.6 6.8 %collective-permute-start.2 = (bf16[24,8,512]{2,1,0:T(8,128)(2,1)S(1)}, bf16[24,8,512]{2,1,0:T(8,128)(2,1)S(1)}, u32[]{:S(2)}, u32[]{:S(2)}) collective-permute-start(bf16[24,8,512]{2,1,0:T(8,128)(2,1)S(1)} %get-tuple-element.48), channel_id=1, source_target_pairs={{0,1},{1,2},{2,3},{4,5},{5,6},{6,7},{8,9},{9,10},{10,11},{12,13},{... | collective-permute-start | bytes 589832 | tf_op jit(solution)/shard_map/ppermute | solution.py:25
  31.9 7.4 %collective-permute-start.3 = (bf16[24,8,512]{2,1,0:T(8,128)(2,1)S(1)}, bf16[24,8,512]{2,1,0:T(8,128)(2,1)S(1)}, u32[]{:S(2)}, u32[]{:S(2)}) collective-permute-start(bf16[24,8,512]{2,1,0:T(8,128)(2,1)S(1)} %get-tuple-element.49), channel_id=1, source_target_pairs={{1,0},{2,1},{3,2},{5,4},{6,5},{7,6},{9,8},{10,9},{11,10},{13,12},{... | collective-permute-start | bytes 589832 | tf_op jit(solution)/shard_map/ppermute | solution.py:27
  56.6 7.7 %collective-permute-start.4 = (bf16[4,16,512]{2,1,0:T(8,128)(2,1)S(1)}, bf16[4,16,512]{2,1,0:T(8,128)(2,1)S(1)}, u32[]{:S(2)}, u32[]{:S(2)}) collective-permute-start(bf16[4,16,512]{2,1,0:T(8,128)(2,1)S(1)} %get-tuple-element.52), channel_id=1, source_target_pairs={{0,4},{4,8},{8,12},{12,16},{16,20},{20,24},{24,28},{1,5},{5,9},{9,... | collective-permute-start | bytes 196616 | tf_op jit(solution)/shard_map/ppermute | solution.py:25
  61.6 6.5 %collective-permute-start.5 = (bf16[4,16,512]{2,1,0:T(8,128)(2,1)S(1)}, bf16[4,16,512]{2,1,0:T(8,128)(2,1)S(1)}, u32[]{:S(2)}, u32[]{:S(2)}) collective-permute-start(bf16[4,16,512]{2,1,0:T(8,128)(2,1)S(1)} %get-tuple-element.53), channel_id=1, source_target_pairs={{4,0},{8,4},{12,8},{16,12},{20,16},{24,20},{28,24},{5,1},{9,5},{13... | collective-permute-start | bytes 196616 | tf_op jit(solution)/shard_map/ppermute | solution.py:27
  68.1 5.6 %collective-permute-start.6 = (bf16[16,4,512]{2,1,0:T(4,128)(2,1)S(1)}, bf16[16,4,512]{2,1,0:T(4,128)(2,1)S(1)}, u32[]{:S(2)}, u32[]{:S(2)}) collective-permute-start(bf16[16,4,512]{2,1,0:T(4,128)(2,1)S(1)} %get-tuple-element.50), channel_id=1, source_target_pairs={{0,1},{1,2},{2,3},{4,5},{5,6},{6,7},{8,9},{9,10},{10,11},{12,13},{... | collective-permute-start | bytes 196616 | tf_op jit(solution)/shard_map/ppermute | solution.py:25
  71.3 5.0 %collective-permute-start.7 = (bf16[16,4,512]{2,1,0:T(4,128)(2,1)S(1)}, bf16[16,4,512]{2,1,0:T(4,128)(2,1)S(1)}, u32[]{:S(2)}, u32[]{:S(2)}) collective-permute-start(bf16[16,4,512]{2,1,0:T(4,128)(2,1)S(1)} %get-tuple-element.51), channel_id=1, source_target_pairs={{1,0},{2,1},{3,2},{5,4},{6,5},{7,6},{9,8},{10,9},{11,10},{13,12},{... | collective-permute-start | bytes 196616 | tf_op jit(solution)/shard_map/ppermute | solution.py:27
  192.5 6.3 %copy-start = (bf16[3,8,16,512]{3,2,1,0:T(8,128)(2,1)S(1)}, bf16[3,8,16,512]{3,2,1,0:T(8,128)(2,1)}, u32[]{:S(2)}) copy-start(bf16[3,8,16,512]{3,2,1,0:T(8,128)(2,1)} %param.10) | copy-start | bytes 1179652
  250.7 6.3 %collective-permute-start.8 = (bf16[3,4,16,512]{3,2,1,0:T(8,128)(2,1)S(1)}, bf16[3,4,16,512]{3,2,1,0:T(8,128)(2,1)S(1)}, u32[]{:S(2)}, u32[]{:S(2)}) collective-permute-start(bf16[3,4,16,512]{3,2,1,0:T(8,128)(2,1)S(1)} %get-tuple-element.46), channel_id=1, source_target_pairs={{0,4},{4,8},{8,12},{12,16},{16,20},{20,24},{24,28},{1,5},{5,9},{9,... | collective-permute-start | bytes 589832 | tf_op jit(solution)/shard_map/ppermute | solution.py:25
  254.0 7.9 %collective-permute-start.9 = (bf16[3,4,16,512]{3,2,1,0:T(8,128)(2,1)S(1)}, bf16[3,4,16,512]{3,2,1,0:T(8,128)(2,1)S(1)}, u32[]{:S(2)}, u32[]{:S(2)}) collective-permute-start(bf16[3,4,16,512]{3,2,1,0:T(8,128)(2,1)S(1)} %get-tuple-element.47), channel_id=1, source_target_pairs={{4,0},{8,4},{12,8},{16,12},{20,16},{24,20},{28,24},{5,1},{9,5},{13... | collective-permute-start | bytes 589832 | tf_op jit(solution)/shard_map/ppermute | solution.py:27
  262.1 6.7 %collective-permute-start.10 = (bf16[3,16,4,512]{3,2,1,0:T(4,128)(2,1)S(1)}, bf16[3,16,4,512]{3,2,1,0:T(4,128)(2,1)S(1)}, u32[]{:S(2)}, u32[]{:S(2)}) collective-permute-start(bf16[3,16,4,512]{3,2,1,0:T(4,128)(2,1)S(1)} %get-tuple-element.25), channel_id=1, source_target_pairs={{0,1},{1,2},{2,3},{4,5},{5,6},{6,7},{8,9},{9,10},{10,11},{12,13},{... | collective-permute-start | bytes 589832 | tf_op jit(solution)/shard_map/ppermute | solution.py:25
  265.3 6.5 %collective-permute-start.11 = (bf16[3,16,4,512]{3,2,1,0:T(4,128)(2,1)S(1)}, bf16[3,16,4,512]{3,2,1,0:T(4,128)(2,1)S(1)}, u32[]{:S(2)}, u32[]{:S(2)}) collective-permute-start(bf16[3,16,4,512]{3,2,1,0:T(4,128)(2,1)S(1)} %get-tuple-element.26), channel_id=1, source_target_pairs={{1,0},{2,1},{3,2},{5,4},{6,5},{7,6},{9,8},{10,9},{11,10},{13,12},{... | collective-permute-start | bytes 589832 | tf_op jit(solution)/shard_map/ppermute | solution.py:27
where the time goes:
time: 442 us; the launch traced here: 435 us
  other arithmetic  353 us (80%)
  starting transfers between devices  31.9 us (7%)
  waiting for transfers between devices  21.4 us (5%)
  local copies, waits for them, and re-layouts  18.3 us (4%)
  between operations  10.4 us (2%)
    add x36, other arithmetic, conv_valid(): total + kernel[tap] * lax.slice_in_dim(values, tap, tap + length, axis=axis)  226 us
    div x3, other arithmetic, local(): back = back / RANK  55.4 us
    another operation x4, other arithmetic, local(): jnp.stack(ratios, axis=0)  51.8 us
    ppermute x6, starting transfers between devices, extended(): lax.ppermute(tail, axis, [(i, (i + 1) % count) for i in range(ends)])  21.6 us
    ppermute x6, waiting for transfers between devices, extended(): lax.ppermute(head, axis, [((i + 1) % count, i) for i in range(ends)])  18.1 us
    add x7, other arithmetic, tv_pass(): return field + TAU * total  12.4 us
    ppermute x6, starting transfers between devices, extended(): lax.ppermute(head, axis, [((i + 1) % count, i) for i in range(ends)])  10.3 us
  transfers between devices with their start and end apart: 12, of which 7 were waited for; matrix products, arithmetic and copies ran while one was open for 4% of the time, Pallas kernels for 0%

commit v1 on v0

v1 whole, which is shorter than its diff:
```python
import functools

import jax
import jax.numpy as jnp
import numpy as np
from jax import lax
from jax.experimental import pallas as pl
from jax.experimental.pallas import tpu as pltpu

VIEWS = 3
RANK = 3
RADIUS = 4
TAPS = 9
PASSES = 8
EPS_TV = 0.25
TAU = 0.08
BACKGROUND = 0.1
CZ, CX = 8, 16
ROWS = CZ * CX
FULL = (CZ + 2 * RADIUS) * (CX + 2 * RADIUS)
DIRS = [(-1, 0), (1, 0), (0, -1), (0, 1), (-1, -1), (-1, 1), (1, -1), (1, 1)]
BF = jnp.bfloat16
F32 = jnp.float32
SPOT = {
    (-1, 0): (128, 64),
    (1, 0): (192, 64),
    (0, -1): (256, 32),
    (0, 1): (288, 32),
    (-1, -1): (320, 16),
    (-1, 1): (336, 16),
    (1, -1): (352, 16),
    (1, 1): (368, 16),
}


def row_places():
    z = np.zeros(FULL, np.int32)
    x = np.zeros(FULL, np.int32)
    z_of = {-1: range(-RADIUS, 0), 0: range(CZ), 1: range(CZ, CZ + RADIUS)}
    x_of = {-1: range(-RADIUS, 0), 0: range(CX), 1: range(CX, CX + RADIUS)}
    for (dz, dx), (first, _) in [((0, 0), (0, 0))] + list(SPOT.items()):
        at = first
        for zi in z_of[dz]:
            for xi in x_of[dx]:
                z[at], x[at] = zi, xi
                at += 1
    tap_z = z[None] - np.arange(CZ, dtype=np.int32)[:, None] + RADIUS
    tap_x = x[None] - np.arange(CX, dtype=np.int32)[:, None] + RADIUS
    return np.concatenate([tap_z, tap_x], axis=0)


def flux(diff):
    return diff * lax.rsqrt(diff * diff + EPS_TV)


def kernel(
    sizes, taps, shift, inter, est, obs, places, out,
    own1, strip1, got1, nat, u, pack, f2, x2, f3, x3, w_f, w_a, c_f, c_a, obs_r, tmp, img, corr,
    sems1, semr1, sems2, semr2, sems3, semr3,
):
    nz, nx = sizes
    iz, ix = lax.axis_index("bz"), lax.axis_index("bxy")
    ny = est.shape[2]

    def exists(d):
        dz, dx = d
        ok = None
        for step, at, count in ((dz, iz, nz), (dx, ix, nx)):
            if step:
                here = at > 0 if step < 0 else at < count - 1
                ok = here if ok is None else jnp.logical_and(ok, here)
        return ok

    def peer(d):
        return {"bz": iz + d[0], "bxy": ix + d[1]}

    def opposite(d):
        return (-d[0], -d[1])

    barrier = pltpu.get_barrier_semaphore()
    for d in DIRS:
        @pl.when(exists(d))
        def _():
            pl.semaphore_signal(barrier, inc=1, device_id=peer(d), device_id_type=pl.DeviceIdType.MESH)

    own1[...] = est[...].astype(BF)
    for side in range(2):
        part = est[:, 8 * side:8 * side + 8, :]
        strip1[side] = part.reshape(4, 16, ny).astype(BF)
    for n, d in enumerate(DIRS):
        @pl.when(jnp.logical_not(exists(d)))
        def _():
            got1[n] = jnp.zeros(got1.shape[1:], BF)
            first, rows = SPOT[d]
            zero = jnp.zeros((rows, ny), BF)
            f2[first:first + rows] = zero
            for v in range(VIEWS):
                f3[v, first:first + rows] = zero

    wide_z = 3 - jnp.where(iz == 0, 1, 0) - jnp.where(iz == nz - 1, 1, 0)
    wide_x = 3 - jnp.where(ix == 0, 1, 0) - jnp.where(ix == nx - 1, 1, 0)
    pl.semaphore_wait(barrier, wide_z * wide_x - 1)

    def round1(n):
        d = DIRS[n]
        there = DIRS.index(opposite(d))
        if d[1] == 0:
            src, dst = own1, got1.at[there]
        else:
            src, dst = strip1.at[0 if d[1] < 0 else 1], got1.at[there, 0:4]
        return pltpu.make_async_remote_copy(
            src_ref=src, dst_ref=dst, send_sem=sems1.at[n], recv_sem=semr1.at[n],
            device_id=peer(d), device_id_type=pl.DeviceIdType.MESH)

    def round23(n, field, strips, send_sem, recv_sem):
        d = DIRS[n]
        first, rows = SPOT[opposite(d)]
        if d[1] == 0:
            src = field.at[0:64] if d[0] < 0 else field.at[64:128]
        else:
            side = 0 if d[1] < 0 else 1
            low = 0 if d[0] <= 0 else 16
            src = strips.at[side, low:low + rows]
        return pltpu.make_async_remote_copy(
            src_ref=src, dst_ref=field.at[first:first + rows], send_sem=send_sem, recv_sem=recv_sem,
            device_id=peer(d), device_id_type=pl.DeviceIdType.MESH)

    def start(copy_of):
        for n, d in enumerate(DIRS):
            @pl.when(exists(d))
            def _():
                copy_of(n).start()

    def finish_send(copy_of):
        for n, d in enumerate(DIRS):
            @pl.when(exists(d))
            def _():
                copy_of(n).wait_send()

    def finish_recv(copy_of):
        for n, d in enumerate(DIRS):
            @pl.when(exists(opposite(d)))
            def _():
                copy_of(n).wait_recv()

    start(round1)

    lane = lax.broadcasted_iota(jnp.int32, (8, ny), 1)
    tap_z = places[0:CZ]
    tap_x = places[CZ:CZ + CX]

    def prepare(v, carry):
        moved = (lane + shift[v]) & (ny - 1)
        for r in range(RANK):
            sums = []
            for axis in range(3):
                base = ((v * RANK + r) * 3 + axis) * TAPS
                total = taps[base]
                for t in range(1, TAPS):
                    total = total + taps[base + t]
                sums.append(total)
            base = (v * RANK + r) * 3 * TAPS
            for w, forward in ((w_f, True), (w_a, False)):
                a = jnp.zeros((CZ, FULL), F32)
                b = jnp.zeros((CX, FULL), F32)
                for t in range(TAPS):
                    at = t if forward else TAPS - 1 - t
                    a = jnp.where(tap_z == t, taps[base + at], a)
                    b = jnp.where(tap_x == t, taps[base + TAPS + at], b)
                a = a / (sums[0] * RANK)
                b = b / sums[1]
                for zo in range(CZ):
                    whole = a[zo:zo + 1] * b
                    high = whole.astype(BF)
                    rows = pl.ds(r * ROWS + zo * CX, CX)
                    w[v, rows, 0:FULL] = high
                    w[v, rows, FULL:2 * FULL] = (whole - high.astype(F32)).astype(BF)
            scale = 1.0 / jnp.full((8, ny), sums[2], F32)
            for t in range(TAPS):
                value = scale * taps[base + 2 * TAPS + t]
                for c, place in ((c_f, moved - (t - RADIUS)), (c_a, moved + (t - RADIUS))):
                    inside = (place >= 0) & (place < ny)
                    c[v, r * TAPS + t] = jnp.where(inside, value, 0.0)
        back = (ny - shift[v]) & (ny - 1)
        for z in range(CZ):
            obs_r[v, z] = pltpu.roll(obs[v, z].astype(F32), back, 1)
        return carry

    lax.fori_loop(0, VIEWS, prepare, 0)

    finish_recv(round1)

    columns = range(ny // 128)
    for c in columns:
        at = slice(128 * c, 128 * c + 128)
        nat[8:16, c, 8:24] = est[:, :, at]
        nat[0:8, c, 8:24] = got1[0, :, :, at].astype(F32)
        nat[16:24, c, 8:24] = got1[1, :, :, at].astype(F32)
        for n, z0, x0 in ((2, 8, 0), (3, 8, 24), (4, 0, 0), (5, 0, 24), (6, 16, 0), (7, 16, 24)):
            nat[z0:z0 + 8, c, x0:x0 + 8] = got1[n, 0:4, :, at].astype(F32).reshape(8, 8, 128)

    def relayout(z, carry):
        for i in range(4):
            for c in columns:
                u[z, i, :, 128 * c:128 * c + 128] = nat[z, c, pl.ds(i, 8, stride=4), :]
        return carry

    lax.fori_loop(0, 24, relayout, 0)

    sub = lax.broadcasted_iota(jnp.int32, (8, 128), 0)
    low_x = jnp.where(ix == 0, 0.0, 1.0)
    high_x = jnp.where(ix == nx - 1, 0.0, 1.0)
    x_mask = jnp.where(sub == 1, low_x, jnp.where(sub == 5, high_x, 1.0))
    x_mask = jnp.concatenate([x_mask] * (ny // 128), axis=1)
    y_mask = jnp.where(lax.broadcasted_iota(jnp.int32, (8, 128), 1) == 127, 0.0, 1.0)

    def tv(p, carry):
        @pl.when(iz == 0)
        def _():
            u[7] = u[8]

        @pl.when(iz == nz - 1)
        def _():
            u[16] = u[15]

        def plane(z, below):
            here = [u[z, i] for i in range(4)]
            above = [flux(u[z + 1, i] - here[i]) for i in range(4)]
            fx = [flux(here[i + 1] - here[i]) for i in range(3)]
            fx.append(flux(pltpu.roll(here[0], 7, 0) - here[3]) * x_mask)
            fx_low = [pltpu.roll(fx[3], 1, 0)] + fx[:3]
            for i in range(4):
                fy = flux(pltpu.roll(here[i], ny - 1, 1) - here[i])
                fy = jnp.concatenate([fy[:, :ny - 128], fy[:, ny - 128:] * y_mask], axis=1)
                total = (above[i] - below[i]) + (fx[i] - fx_low[i]) + (fy - pltpu.roll(fy, 1, 1))
                u[z, i] = here[i] + TAU * total
            return tuple(above)

        first = tuple(flux(u[p, i] - u[p - 1, i]) for i in range(4))
        lax.fori_loop(p, 24 - p, plane, first)
        return carry

    lax.fori_loop(1, PASSES + 1, tv, 0)
    finish_send(round1)

    def natural(z, carry):
        for i in range(4):
            for c in columns:
                nat[z, c, pl.ds(i, 8, stride=4), :] = u[z, i, :, 128 * c:128 * c + 128]
        return carry

    lax.fori_loop(8, 16, natural, 0)

    def fill(field, strips, read):
        for z in range(CZ):
            field[z * CX:(z + 1) * CX] = read(z).astype(BF)
            pack[0, 4 * z:4 * z + 4] = read(z)[0:4]
            pack[1, 4 * z:4 * z + 4] = read(z)[12:16]
        strips[...] = pack[...].astype(BF)

    fill(f2, x2, lambda z: jnp.concatenate([nat[8 + z, c, 8:24] for c in columns], axis=1))
    round2 = lambda n: round23(n, f2, x2, sems2.at[n], semr2.at[n])
    start(round2)
    finish_recv(round2)

    f2d = jnp.concatenate([f2[0:FULL], f2[0:FULL]], axis=0)

    def along_y(c, v, j, sign):
        parts = [tmp[r, j] for r in range(RANK)]
        total = None
        for t in range(TAPS):
            term = c[v, t] * parts[0]
            for r in range(1, RANK):
                term = term + c[v, r * TAPS + t] * parts[r]
            move = (sign * (t - RADIUS)) % ny
            if move:
                term = pltpu.roll(term, move, 1)
            total = term if total is None else total + term
        return total

    def round3(v):
        return lambda n: round23(n, f3.at[v], x3.at[v], sems3.at[v, n], semr3.at[v, n])

    for v in range(VIEWS):
        tmp[...] = jnp.dot(w_f[v], f2d, preferred_element_type=F32).reshape(tmp.shape)
        flag = inter[(v * nz + iz) * nx + ix]

        def ratios(j, carry):
            image = along_y(c_f, v, j, -1)
            img[j] = jnp.where(flag > 0, obs_r[v, j // 2, pl.ds((j % 2) * 8, 8), :] / (image + BACKGROUND), 1.0)
            return carry

        lax.fori_loop(0, 16, ratios, 0)
        fill(f3.at[v], x3.at[v], lambda z: img[2 * z:2 * z + 2].reshape(CX, ny))
        start(round3(v))
    finish_send(round2)

    for v in range(VIEWS):
        finish_recv(round3(v))
        f3d = jnp.concatenate([f3[v], f3[v]], axis=0)
        tmp[...] = jnp.dot(w_a[v], f3d, preferred_element_type=F32).reshape(tmp.shape)

        def spread(j, carry):
            back = along_y(c_a, v, j, 1)
            if v:
                back = back + corr[j]
            if v < VIEWS - 1:
                corr[j] = back
            else:
                z, x = j // 2, (j % 2) * 8
                smoothed = jnp.concatenate([nat[8 + z, c, pl.ds(8 + x, 8)] for c in columns], axis=1)
                out[z, pl.ds(x, 8), :] = smoothed * back / VIEWS
            return carry

        lax.fori_loop(0, 16, spread, 0)
    for v in range(VIEWS):
        finish_send(round3(v))


def local(sizes, estimate, observed, psf_taps, view_shift, intersection):
    cz, cx, ny = estimate.shape
    places = jnp.asarray(row_places())
    vmem = pl.BlockSpec(memory_space=pltpu.VMEM)
    smem = pl.BlockSpec(memory_space=pltpu.SMEM)
    dma = pltpu.SemaphoreType.DMA
    return pl.pallas_call(
        functools.partial(kernel, sizes),
        out_shape=jax.ShapeDtypeStruct((cz, cx, ny), F32),
        in_specs=[smem, smem, smem, vmem, vmem, vmem],
        out_specs=vmem,
        scratch_shapes=[
            pltpu.VMEM((cz, cx, ny), BF),
            pltpu.VMEM((2, 4, 16, ny), BF),
            pltpu.VMEM((8, 8, 16, ny), BF),
            pltpu.VMEM((24, ny // 128, 32, 128), F32),
            pltpu.VMEM((24, 4, 8, ny), F32),
            pltpu.VMEM((2, 32, ny), F32),
            pltpu.VMEM((FULL, ny), BF),
            pltpu.VMEM((2, 32, ny), BF),
            pltpu.VMEM((VIEWS, FULL, ny), BF),
            pltpu.VMEM((VIEWS, 2, 32, ny), BF),
            pltpu.VMEM((VIEWS, RANK * ROWS, 2 * FULL), BF),
            pltpu.VMEM((VIEWS, RANK * ROWS, 2 * FULL), BF),
            pltpu.VMEM((VIEWS, RANK * TAPS, 8, ny), F32),
            pltpu.VMEM((VIEWS, RANK * TAPS, 8, ny), F32),
            pltpu.VMEM((VIEWS, cz, cx, ny), F32),
            pltpu.VMEM((RANK, 16, 8, ny), F32),
            pltpu.VMEM((16, 8, ny), F32),
            pltpu.VMEM((16, 8, ny), F32),
            dma((8,)), dma((8,)), dma((8,)), dma((8,)), dma((VIEWS, 8)), dma((VIEWS, 8)),
        ],
        compiler_params=pltpu.CompilerParams(
            collective_id=0, has_side_effects=True, vmem_limit_bytes=56 * 1024 * 1024),
        cost_estimate=pl.CostEstimate(flops=10**9, bytes_accessed=10**6, transcendentals=5 * 10**6),
    )(psf_taps.reshape(-1), view_shift, intersection.reshape(-1), estimate, observed, places)


def solution(mesh):
    from jax.sharding import PartitionSpec as P
    sizes = (mesh.shape["bz"], mesh.shape["bxy"])
    return jax.shard_map(
        functools.partial(local, sizes),
        mesh=mesh,
        in_specs=(P("bz", "bxy", None), P(None, "bz", "bxy", None), P(), P(), P()),
        out_specs=P("bz", "bxy", None),
        check_vma=False,
    )
```

time: 442 us -> 57.3 us (0.13)
  the two profiles are of different devices: /device:TPU:3 before, /device:TPU:11 now
where the time goes in v1:
time: 57.3 us; the launch traced here: 57.1 us
  Pallas kernels  53.3 us (93%)
  local copies, waits for them, and re-layouts  3.8 us (7%)
    pallas_call x1, Pallas kernels, local(): pl.pallas_call(functools.partial(kernel, sizes), out_shape=jax.ShapeDtype...  53.3 us
    unnamed x4, local copies, waits for them, and re-layouts  1.77 us
    reshape x1, local copies, waits for them, and re-layouts, local(): psf_taps.reshape(-1)  1.4 us

profile of v1, /device:TPU:11, one launch (start us, length us, event | category | flops | bytes accessed | tf_op | source)
XLA Modules:
  0.0 57.1 jit_solution(13349131345366926725)
XLA Ops:
  0.0 0.0 copy-start
  0.0 1.4 %reshape.6.taps = f32[243]{0:T(256)} reshape(f32[3,3,3,9]{3,2,1,0:T(4,128)} %param.8) | data formatting | bytes 1944 | tf_op jit(solution)/shard_map/reshape | solution.py:355
  1.4 0.0 copy-done
  1.4 0.1 copy.8
  1.5 0.6 %reshape.7.inter = s32[96]{0:T(128)} reshape(s32[3,8,4]{2,1,0:T(8,128)S(1)} %copy.8) | data formatting | bytes 768 | tf_op jit(solution)/shard_map/reshape | solution.py:355
  2.1 53.3 %shard_map.64 = f32[8,16,512]{2,1,0:T(8,128)} custom-call(f32[243]{0:T(256)} %reshape.6.taps, s32[3]{0:T(128)} %shift.1, s32[96]{0:T(128)} %reshape.7.inter, f32[8,16,512]{2,1,0:T(8,128)} %est.1, bf16[3,8,16,512]{3,2,1,0:T(8,128)(2,1)} %obs.1, s32[24,384]{1,0:T(8,128)} %constant.2.clone.places), custom_call_target="tpu_custom_call" | custom-call | flops 1000000000 | bytes 1000000 | tf_op jit(solution)/shard_map/pallas_call | solution.py:326
  55.5 1.7 %copy.10 = f32[8,16,512]{2,1,0:T(8,128)} copy(f32[8,16,512]{2,1,0:T(8,128)} %shard_map.64) | data formatting | bytes 524288
Async XLA Ops:
  0.0 1.4 %copy-start = (s32[3,8,4]{1,2,0:T(4,128)S(1)}, s32[3,8,4]{1,2,0:T(4,128)}, u32[]{:S(2)}) copy-start(s32[3,8,4]{1,2,0:T(4,128)} %param.10) | copy-start | bytes 1156

commit v2 on v1

v2 whole, which is shorter than its diff:
```python
import functools

import jax
import jax.numpy as jnp
import numpy as np
from jax import lax
from jax.experimental import pallas as pl
from jax.experimental.pallas import tpu as pltpu

VIEWS = 3
RANK = 3
RADIUS = 4
TAPS = 9
PASSES = 8
ROUNDS = 3 + VIEWS
EPS_TV = 0.25
TAU = 0.08
BACKGROUND = 0.1
CZ, CX = 8, 16
ROWS = CZ * CX
FULL = (CZ + 2 * RADIUS) * (CX + 2 * RADIUS)
DIRS = [(-1, 0), (1, 0), (0, -1), (0, 1), (-1, -1), (-1, 1), (1, -1), (1, 1)]
BF = jnp.bfloat16
F32 = jnp.float32
SPOT = {
    (-1, 0): (128, 64),
    (1, 0): (192, 64),
    (0, -1): (256, 32),
    (0, 1): (288, 32),
    (-1, -1): (320, 16),
    (-1, 1): (336, 16),
    (1, -1): (352, 16),
    (1, 1): (368, 16),
}


def row_places():
    z = np.zeros(FULL, np.int32)
    x = np.zeros(FULL, np.int32)
    z_of = {-1: range(-RADIUS, 0), 0: range(CZ), 1: range(CZ, CZ + RADIUS)}
    x_of = {-1: range(-RADIUS, 0), 0: range(CX), 1: range(CX, CX + RADIUS)}
    for (dz, dx), (first, _) in [((0, 0), (0, 0))] + list(SPOT.items()):
        at = first
        for zi in z_of[dz]:
            for xi in x_of[dx]:
                z[at], x[at] = zi, xi
                at += 1
    tap_z = z[None] - np.arange(CZ, dtype=np.int32)[:, None] + RADIUS
    tap_x = x[None] - np.arange(CX, dtype=np.int32)[:, None] + RADIUS
    return np.concatenate([tap_z, tap_x], axis=0)


def flux(diff):
    return diff * lax.rsqrt(diff * diff + EPS_TV)


def kernel(
    sizes, taps, shift, inter, est, obs, places, out,
    nat, u, pack, fields, strips, w_f, w_a, c_f, c_a, obs_r, tmp, img, corr, send_sems, recv_sems,
):
    nz, nx = sizes
    iz, ix = lax.axis_index("bz"), lax.axis_index("bxy")
    ny = est.shape[2]

    def exists(d):
        dz, dx = d
        ok = None
        for step, at, count in ((dz, iz, nz), (dx, ix, nx)):
            if step:
                here = at > 0 if step < 0 else at < count - 1
                ok = here if ok is None else jnp.logical_and(ok, here)
        return ok

    def peer(d):
        return {"bz": iz + d[0], "bxy": ix + d[1]}

    def opposite(d):
        return (-d[0], -d[1])

    barrier = pltpu.get_barrier_semaphore()
    for d in DIRS:
        @pl.when(exists(d))
        def _():
            pl.semaphore_signal(barrier, inc=1, device_id=peer(d), device_id_type=pl.DeviceIdType.MESH)

    for d in DIRS:
        @pl.when(jnp.logical_not(exists(d)))
        def _():
            first, rows = SPOT[d]
            for k in range(ROUNDS):
                fields[k, first:first + rows] = jnp.zeros((rows, ny), BF)

    def fill(k, read):
        for z in range(CZ):
            fields[k, z * CX:(z + 1) * CX] = read(z).astype(BF)
            pack[0, 4 * z:4 * z + 4] = read(z)[0:4]
            pack[1, 4 * z:4 * z + 4] = read(z)[12:16]
        strips[k] = pack[...].astype(BF)

    fill(0, lambda z: est[z])

    wide_z = 3 - jnp.where(iz == 0, 1, 0) - jnp.where(iz == nz - 1, 1, 0)
    wide_x = 3 - jnp.where(ix == 0, 1, 0) - jnp.where(ix == nx - 1, 1, 0)
    pl.semaphore_wait(barrier, wide_z * wide_x - 1)

    def copy_of(k, n):
        d = DIRS[n]
        first, rows = SPOT[opposite(d)]
        if d[1] == 0:
            low = 0 if d[0] < 0 else 64
            src = fields.at[k, low:low + 64]
        else:
            side = 0 if d[1] < 0 else 1
            low = 0 if d[0] <= 0 else 16
            src = strips.at[k, side, low:low + rows]
        return pltpu.make_async_remote_copy(
            src_ref=src, dst_ref=fields.at[k, first:first + rows],
            send_sem=send_sems.at[k, n], recv_sem=recv_sems.at[k, n],
            device_id=peer(d), device_id_type=pl.DeviceIdType.MESH)

    def start(k):
        for n, d in enumerate(DIRS):
            @pl.when(exists(d))
            def _():
                copy_of(k, n).start()

    def finish_send(k):
        for n, d in enumerate(DIRS):
            @pl.when(exists(d))
            def _():
                copy_of(k, n).wait_send()

    def finish_recv(k):
        for n, d in enumerate(DIRS):
            @pl.when(exists(opposite(d)))
            def _():
                copy_of(k, n).wait_recv()

    start(0)

    lane = lax.broadcasted_iota(jnp.int32, (8, ny), 1)
    tap_z = places[0:CZ]
    tap_x = places[CZ:CZ + CX]

    def prepare(v):
        moved = (lane + shift[v]) & (ny - 1)
        for r in range(RANK):
            sums = []
            for axis in range(3):
                total = taps[v, r, axis, 0]
                for t in range(1, TAPS):
                    total = total + taps[v, r, axis, t]
                sums.append(total)
            for w, forward in ((w_f, True), (w_a, False)):
                a = jnp.zeros((CZ, FULL), F32)
                b = jnp.zeros((CX, FULL), F32)
                for t in range(TAPS):
                    at = t if forward else TAPS - 1 - t
                    a = jnp.where(tap_z == t, taps[v, r, 0, at], a)
                    b = jnp.where(tap_x == t, taps[v, r, 1, at], b)
                a = a / (sums[0] * RANK)
                b = b / sums[1]
                for zo in range(CZ):
                    whole = a[zo:zo + 1] * b
                    high = whole.astype(BF)
                    rows = pl.ds(r * ROWS + zo * CX, CX)
                    w[v, rows, 0:FULL] = high
                    w[v, rows, FULL:2 * FULL] = (whole - high.astype(F32)).astype(BF)
            scale = 1.0 / jnp.full((8, ny), sums[2], F32)
            for t in range(TAPS):
                value = scale * taps[v, r, 2, t]
                for c, place in ((c_f, moved - (t - RADIUS)), (c_a, moved + (t - RADIUS))):
                    inside = (place >= 0) & (place < ny)
                    c[v, r * TAPS + t] = jnp.where(inside, value, 0.0)
        back = (ny - shift[v]) & (ny - 1)
        for z in range(CZ):
            obs_r[v, z] = pltpu.roll(obs[v, z].astype(F32), back, 1)

    prepare(0)
    finish_recv(0)

    columns = range(ny // 128)
    for c in columns:
        nat[4:12, c, 8:24] = est[:, :, 128 * c:128 * c + 128]

    def assemble(k):
        for c in columns:
            at = slice(128 * c, 128 * c + 128)
            for dz, dx in DIRS:
                first, rows = SPOT[(dz, dx)]
                piece = fields[k, first:first + rows, at].astype(F32)
                z0 = {-1: 0, 0: 4, 1: 12}[dz]
                if dx == 0:
                    nat[z0:z0 + 4, c, 8:24] = piece.reshape(4, 16, 128)
                else:
                    x0 = 4 if dx < 0 else 24
                    for z in range(rows // 4):
                        nat[z0 + z, c, x0:x0 + 4] = piece[4 * z:4 * z + 4]

        def relayout(z, carry):
            for i in range(3):
                for c in columns:
                    u[z, i, :, 128 * c:128 * c + 128] = nat[z, c, pl.ds(4 + i, 8, stride=3), :]
            return carry

        lax.fori_loop(0, 16, relayout, 0)

    sub = lax.broadcasted_iota(jnp.int32, (8, 128), 0)
    low_x = jnp.where(ix == 0, 0.0, 1.0)
    high_x = jnp.where(ix == nx - 1, 0.0, 1.0)
    masks = []
    for at, keep in ((1, low_x), (6, high_x)):
        masks.append(jnp.concatenate([jnp.where(sub == at, keep, 1.0)] * (ny // 128), axis=1))
    y_mask = jnp.where(lax.broadcasted_iota(jnp.int32, (8, 128), 1) == 127, 0.0, 1.0)

    def tv(p, carry):
        @pl.when(iz == 0)
        def _():
            u[3] = u[4]

        @pl.when(iz == nz - 1)
        def _():
            u[12] = u[11]

        def plane(z, below):
            here = [u[z, i] for i in range(3)]
            above = [flux(u[z + 1, i] - here[i]) for i in range(3)]
            fx = [flux(here[i + 1] - here[i]) * masks[i] for i in range(2)]
            fx.append(flux(pltpu.roll(here[0], 7, 0) - here[2]))
            fx_low = [pltpu.roll(fx[2], 1, 0)] + fx[:2]
            for i in range(3):
                fy = flux(pltpu.roll(here[i], ny - 1, 1) - here[i])
                fy = jnp.concatenate([fy[:, :ny - 128], fy[:, ny - 128:] * y_mask], axis=1)
                total = (above[i] - below[i]) + (fx[i] - fx_low[i]) + (fy - pltpu.roll(fy, 1, 1))
                u[z, i] = here[i] + TAU * total
            return tuple(above)

        first = tuple(flux(u[p, i] - u[p - 1, i]) for i in range(3))
        lax.fori_loop(p, 16 - p, plane, first)
        return carry

    def natural(z, carry):
        for i in range(3):
            for c in columns:
                nat[z, c, pl.ds(4 + i, 8, stride=3), :] = u[z, i, :, 128 * c:128 * c + 128]
        return carry

    for half in range(2):
        assemble(half)
        lax.fori_loop(1, PASSES // 2 + 1, tv, 0)
        lax.fori_loop(4, 12, natural, 0)
        fill(half + 1, lambda z: jnp.concatenate([nat[4 + z, c, 8:24] for c in columns], axis=1))
        start(half + 1)
        prepare(half + 1)
        finish_recv(half + 1)

    f2d = jnp.concatenate([fields[2], fields[2]], axis=0)

    def along_y(c, v, j, sign):
        parts = [tmp[r, pl.ds(2 * j, 2)] for r in range(RANK)]
        total = None
        for t in range(TAPS):
            term = c[v, t] * parts[0]
            for r in range(1, RANK):
                term = term + c[v, r * TAPS + t] * parts[r]
            move = (sign * (t - RADIUS)) % ny
            if move:
                term = pltpu.roll(term, move, 2)
            total = term if total is None else total + term
        return total

    for v in range(VIEWS):
        tmp[...] = jnp.dot(w_f[v], f2d, preferred_element_type=F32).reshape(tmp.shape)
        flag = inter[v, iz, ix]

        def ratios(j, carry):
            image = along_y(c_f, v, j, -1)
            img[j] = jnp.where(flag > 0, obs_r[v, j] / (image.reshape(CX, ny) + BACKGROUND), 1.0)
            return carry

        lax.fori_loop(0, CZ, ratios, 0)
        fill(3 + v, lambda z: img[z])
        start(3 + v)

    for v in range(VIEWS):
        finish_recv(3 + v)
        f3d = jnp.concatenate([fields[3 + v], fields[3 + v]], axis=0)
        tmp[...] = jnp.dot(w_a[v], f3d, preferred_element_type=F32).reshape(tmp.shape)

        def spread(j, carry):
            back = along_y(c_a, v, j, 1).reshape(CX, ny)
            if v:
                back = back + corr[j]
            if v < VIEWS - 1:
                corr[j] = back
            else:
                smoothed = jnp.concatenate([nat[4 + j, c, 8:24] for c in columns], axis=1)
                out[j] = smoothed * back / VIEWS
            return carry

        lax.fori_loop(0, CZ, spread, 0)
    for k in range(ROUNDS):
        finish_send(k)


def local(sizes, estimate, observed, psf_taps, view_shift, intersection):
    cz, cx, ny = estimate.shape
    places = jnp.asarray(row_places())
    vmem = pl.BlockSpec(memory_space=pltpu.VMEM)
    smem = pl.BlockSpec(memory_space=pltpu.SMEM)
    dma = pltpu.SemaphoreType.DMA
    return pl.pallas_call(
        functools.partial(kernel, sizes),
        out_shape=jax.ShapeDtypeStruct((cz, cx, ny), F32),
        in_specs=[smem, smem, smem, vmem, vmem, vmem],
        out_specs=vmem,
        scratch_shapes=[
            pltpu.VMEM((16, ny // 128, 32, 128), F32),
            pltpu.VMEM((16, 3, 8, ny), F32),
            pltpu.VMEM((2, 32, ny), F32),
            pltpu.VMEM((ROUNDS, FULL, ny), BF),
            pltpu.VMEM((ROUNDS, 2, 32, ny), BF),
            pltpu.VMEM((VIEWS, RANK * ROWS, 2 * FULL), BF),
            pltpu.VMEM((VIEWS, RANK * ROWS, 2 * FULL), BF),
            pltpu.VMEM((VIEWS, RANK * TAPS, 8, ny), F32),
            pltpu.VMEM((VIEWS, RANK * TAPS, 8, ny), F32),
            pltpu.VMEM((VIEWS, cz, cx, ny), F32),
            pltpu.VMEM((RANK, 16, 8, ny), F32),
            pltpu.VMEM((CZ, CX, ny), F32),
            pltpu.VMEM((CZ, CX, ny), F32),
            dma((ROUNDS, 8)), dma((ROUNDS, 8)),
        ],
        compiler_params=pltpu.CompilerParams(
            collective_id=0, has_side_effects=True, vmem_limit_bytes=24 * 1024 * 1024),
        cost_estimate=pl.CostEstimate(flops=10**9, bytes_accessed=10**6, transcendentals=5 * 10**6),
    )(psf_taps, view_shift, intersection, estimate, observed, places)


def solution(mesh):
    from jax.sharding import PartitionSpec as P
    sizes = (mesh.shape["bz"], mesh.shape["bxy"])
    return jax.shard_map(
        functools.partial(local, sizes),
        mesh=mesh,
        in_specs=(P("bz", "bxy", None), P(None, "bz", "bxy", None), P(), P(), P()),
        out_specs=P("bz", "bxy", None),
        check_vma=False,
    )
```

time: 57.3 us -> 50.5 us (0.88)
  Pallas kernels: 53.3 us -> 45.3 us
  local copies, waits for them, and re-layouts: 3.8 us -> 4.86 us
    pallas_call x1, Pallas kernels: 53.3 us -> 45.3 us  [local(): pl.pallas_call(functools.partial(kernel, sizes), out_shape=jax.ShapeDtype...]
    unnamed x4 -> x12, local copies, waits for them, and re-layouts: 1.77 us -> 4.86 us
    reshape x2 -> x0, local copies, waits for them, and re-layouts: 2.04 us -> none  [the longest x1 1.4 us: local(): psf_taps.reshape(-1)]
where the time goes in v2:
time: 50.5 us; the launch traced here: 50.1 us
  Pallas kernels  45.3 us (90%)
  local copies, waits for them, and re-layouts  4.86 us (10%)
    pallas_call x1, Pallas kernels, local(): pl.pallas_call(functools.partial(kernel, sizes), out_shape=jax.ShapeDtype...  45.3 us
    unnamed x12, local copies, waits for them, and re-layouts  4.86 us

profile of v2, /device:TPU:11, one launch (start us, length us, event | category | flops | bytes accessed | tf_op | source)
XLA Modules:
  0.0 50.1 jit_solution(8586424174589449914)
XLA Ops:
  0.0 0.0 copy-start.2
  0.0 0.8 %copy.7.inter = s32[3,8,4]{2,1,0:T(8,128)S(1)} copy(s32[3,8,4]{1,2,0:T(4,128)} %param.10) | data formatting | bytes 768 | tf_op args[4]
  0.8 0.0 copy-done.2
  0.8 0.0 copy-start
  0.8 1.0 %copy-done = bf16[3,8,16,512]{3,2,1,0:T(8,128)(2,1)S(1)} copy-done((bf16[3,8,16,512]{3,2,1,0:T(8,128)(2,1)S(1)}, bf16[3,8,16,512]{3,2,1,0:T(8,128)(2,1)}, u32[]{:S(2)}) %copy-start) | copy-done | bytes 393240
  1.8 0.0 copy-start.1
  1.8 0.9 %copy-done.1 = f32[8,16,512]{2,1,0:T(8,128)S(1)} copy-done((f32[8,16,512]{2,1,0:T(8,128)S(1)}, f32[8,16,512]{2,1,0:T(8,128)}, u32[]{:S(2)}) %copy-start.1) | copy-done | bytes 262168
  2.7 0.0 copy-start.3
  2.7 0.7 %copy-done.3 = s32[3]{0:T(128)S(1)} copy-done((s32[3]{0:T(128)S(1)}, s32[3]{0:T(128)}, u32[]{:S(2)}) %copy-start.3) | copy-done | bytes 36
  3.4 0.0 copy-start.4
  3.4 0.8 %copy-done.4 = s32[24,384]{1,0:T(8,128)S(1)} copy-done((s32[24,384]{1,0:T(8,128)S(1)}, s32[24,384]{1,0:T(8,128)}, u32[]{:S(2)}) %copy-start.4) | copy-done | bytes 36888
  4.2 45.3 %shard_map.64 = f32[8,16,512]{2,1,0:T(8,128)S(1)} custom-call(f32[3,3,3,9]{3,2,1,0:T(4,128)S(1)} %copy-done.2, s32[3]{0:T(128)S(1)} %copy-done.3, s32[3,8,4]{2,1,0:T(8,128)S(1)} %copy.7.inter, f32[8,16,512]{2,1,0:T(8,128)S(1)} %copy-done.1, bf16[3,8,16,512]{3,2,1,0:T(8,128)(2,1)S(1)} %copy-done, s32[24,384]{1,0:T(8,128)S(1)} %copy-done.4), custom_call_target="tpu_custom_call" | custom-call | flops 1000000000 | bytes 1000000 | tf_op jit(solution)/shard_map/pallas_call | solution.py:312
  49.4 0.7 %copy.9 = f32[8,16,512]{2,1,0:T(8,128)} copy(f32[8,16,512]{2,1,0:T(8,128)S(1)} %shard_map.64) | data formatting | bytes 524288
Async XLA Ops:
  0.0 0.8 %copy-start.2 = (f32[3,3,3,9]{3,2,1,0:T(4,128)S(1)}, f32[3,3,3,9]{3,2,1,0:T(4,128)}, u32[]{:S(2)}) copy-start(f32[3,3,3,9]{3,2,1,0:T(4,128)} %taps.1) | copy-start | bytes 2920
  0.8 1.0 %copy-start = (bf16[3,8,16,512]{3,2,1,0:T(8,128)(2,1)S(1)}, bf16[3,8,16,512]{3,2,1,0:T(8,128)(2,1)}, u32[]{:S(2)}) copy-start(bf16[3,8,16,512]{3,2,1,0:T(8,128)(2,1)} %obs.1) | copy-start | bytes 1179652
  1.8 0.9 %copy-start.1 = (f32[8,16,512]{2,1,0:T(8,128)S(1)}, f32[8,16,512]{2,1,0:T(8,128)}, u32[]{:S(2)}) copy-start(f32[8,16,512]{2,1,0:T(8,128)} %est.1) | copy-start | bytes 786436
  2.7 0.7 %copy-start.3 = (s32[3]{0:T(128)S(1)}, s32[3]{0:T(128)}, u32[]{:S(2)}) copy-start(s32[3]{0:T(128)} %shift.1) | copy-start | bytes 40
  3.4 0.8 %copy-start.4 = (s32[24,384]{1,0:T(8,128)S(1)}, s32[24,384]{1,0:T(8,128)}, u32[]{:S(2)}) copy-start(s32[24,384]{1,0:T(8,128)} %constant.2.clone.places) | copy-start | bytes 110596

commit v3 on v2

--- a/solution.py
+++ b/solution.py
@@ -2,7 +2,6 @@
 
 import jax
 import jax.numpy as jnp
-import numpy as np
 from jax import lax
 from jax.experimental import pallas as pl
 from jax.experimental.pallas import tpu as pltpu
@@ -35,19 +34,16 @@
 
 
 def row_places():
-    z = np.zeros(FULL, np.int32)
-    x = np.zeros(FULL, np.int32)
-    z_of = {-1: range(-RADIUS, 0), 0: range(CZ), 1: range(CZ, CZ + RADIUS)}
-    x_of = {-1: range(-RADIUS, 0), 0: range(CX), 1: range(CX, CX + RADIUS)}
-    for (dz, dx), (first, _) in [((0, 0), (0, 0))] + list(SPOT.items()):
-        at = first
-        for zi in z_of[dz]:
-            for xi in x_of[dx]:
-                z[at], x[at] = zi, xi
-                at += 1
-    tap_z = z[None] - np.arange(CZ, dtype=np.int32)[:, None] + RADIUS
-    tap_x = x[None] - np.arange(CX, dtype=np.int32)[:, None] + RADIUS
-    return np.concatenate([tap_z, tap_x], axis=0)
+    k = lax.broadcasted_iota(jnp.int32, (CZ + CX, FULL), 1)
+    z, x = k // CX, k % CX
+    for (dz, dx), (first, rows) in SPOT.items():
+        q = k - first
+        wide = CX if dx == 0 else RADIUS
+        here = (q >= 0) & (q < rows)
+        z = jnp.where(here, q // wide + (-RADIUS, 0, CZ)[dz + 1], z)
+        x = jnp.where(here, q % wide + (-RADIUS, 0, CX)[dx + 1], x)
+    row = lax.broadcasted_iota(jnp.int32, (CZ + CX, FULL), 0)
+    return jnp.where(row < CZ, z - row, x - row + CZ) + RADIUS
 
 
 def flux(diff):
@@ -55,12 +51,20 @@
 
 
 def kernel(
-    sizes, taps, shift, inter, est, obs, places, out,
-    nat, u, pack, fields, strips, w_f, w_a, c_f, c_a, obs_r, tmp, img, corr, send_sems, recv_sems,
+    sizes, taps_in, shift_in, inter_in, est_in, obs_in, out,
+    nat, u, pack, fields, strips, w_f, w_a, c_f, c_a, obs_r, tmp, img, corr,
+    taps, shift, inter, est, obs, send_sems, recv_sems, in_sems,
 ):
     nz, nx = sizes
     iz, ix = lax.axis_index("bz"), lax.axis_index("bxy")
     ny = est.shape[2]
+    loads = [
+        pltpu.make_async_copy(a, b, in_sems.at[n])
+        for n, (a, b) in enumerate(
+            ((est_in, est), (taps_in, taps), (shift_in, shift), (inter_in, inter), (obs_in, obs)))
+    ]
+    for load in loads:
+        load.start()
 
     def exists(d):
         dz, dx = d
@@ -97,6 +101,7 @@
             pack[1, 4 * z:4 * z + 4] = read(z)[12:16]
         strips[k] = pack[...].astype(BF)
 
+    loads[0].wait()
     fill(0, lambda z: est[z])
 
     wide_z = 3 - jnp.where(iz == 0, 1, 0) - jnp.where(iz == nz - 1, 1, 0)
@@ -139,6 +144,7 @@
     start(0)
 
     lane = lax.broadcasted_iota(jnp.int32, (8, ny), 1)
+    places = row_places()
     tap_z = places[0:CZ]
     tap_x = places[CZ:CZ + CX]
 
@@ -176,6 +182,8 @@
         for z in range(CZ):
             obs_r[v, z] = pltpu.roll(obs[v, z].astype(F32), back, 1)
 
+    for load in loads[1:]:
+        load.wait()
     prepare(0)
     finish_recv(0)
 
@@ -213,7 +221,7 @@
         masks.append(jnp.concatenate([jnp.where(sub == at, keep, 1.0)] * (ny // 128), axis=1))
     y_mask = jnp.where(lax.broadcasted_iota(jnp.int32, (8, 128), 1) == 127, 0.0, 1.0)
 
-    def tv(p, carry):
+    def tv(p):
         @pl.when(iz == 0)
         def _():
             u[3] = u[4]
@@ -222,22 +230,26 @@
         def _():
             u[12] = u[11]
 
-        def plane(z, below):
-            here = [u[z, i] for i in range(3)]
-            above = [flux(u[z + 1, i] - here[i]) for i in range(3)]
-            fx = [flux(here[i + 1] - here[i]) * masks[i] for i in range(2)]
-            fx.append(flux(pltpu.roll(here[0], 7, 0) - here[2]))
-            fx_low = [pltpu.roll(fx[2], 1, 0)] + fx[:2]
-            for i in range(3):
-                fy = flux(pltpu.roll(here[i], ny - 1, 1) - here[i])
-                fy = jnp.concatenate([fy[:, :ny - 128], fy[:, ny - 128:] * y_mask], axis=1)
-                total = (above[i] - below[i]) + (fx[i] - fx_low[i]) + (fy - pltpu.roll(fy, 1, 1))
-                u[z, i] = here[i] + TAU * total
-            return tuple(above)
+        def planes(step, below):
+            z0 = p + step * (8 - p)
+            below = list(below)
+            here = [u[z0, i] for i in range(3)]
+            for z in range(8 - p):
+                after = [u[z0 + z + 1, i] for i in range(3)]
+                above = [flux(after[i] - here[i]) for i in range(3)]
+                fx = [flux(here[i + 1] - here[i]) * masks[i] for i in range(2)]
+                fx.append(flux(pltpu.roll(here[0], 7, 0) - here[2]))
+                fx_low = [pltpu.roll(fx[2], 1, 0)] + fx[:2]
+                for i in range(3):
+                    fy = flux(pltpu.roll(here[i], ny - 1, 1) - here[i])
+                    fy = jnp.concatenate([fy[:, :ny - 128], fy[:, ny - 128:] * y_mask], axis=1)
+                    total = (above[i] - below[i]) + (fx[i] - fx_low[i]) + (fy - pltpu.roll(fy, 1, 1))
+                    u[z0 + z, i] = here[i] + TAU * total
+                here, below = after, above
+            return tuple(below)
 
         first = tuple(flux(u[p, i] - u[p - 1, i]) for i in range(3))
-        lax.fori_loop(p, 16 - p, plane, first)
-        return carry
+        lax.fori_loop(0, 2, planes, first)
 
     def natural(z, carry):
         for i in range(3):
@@ -247,7 +259,8 @@
 
     for half in range(2):
         assemble(half)
-        lax.fori_loop(1, PASSES // 2 + 1, tv, 0)
+        for p in range(1, PASSES // 2 + 1):
+            tv(p)
         lax.fori_loop(4, 12, natural, 0)
         fill(half + 1, lambda z: jnp.concatenate([nat[4 + z, c, 8:24] for c in columns], axis=1))
         start(half + 1)
@@ -271,14 +284,14 @@
 
     for v in range(VIEWS):
         tmp[...] = jnp.dot(w_f[v], f2d, preferred_element_type=F32).reshape(tmp.shape)
-        flag = inter[v, iz, ix]
+        flag = inter[v, ix, iz]
 
         def ratios(j, carry):
             image = along_y(c_f, v, j, -1)
             img[j] = jnp.where(flag > 0, obs_r[v, j] / (image.reshape(CX, ny) + BACKGROUND), 1.0)
             return carry
 
-        lax.fori_loop(0, CZ, ratios, 0)
+        lax.fori_loop(0, CZ, ratios, 0, unroll=2)
         fill(3 + v, lambda z: img[z])
         start(3 + v)
 
@@ -298,21 +311,21 @@
                 out[j] = smoothed * back / VIEWS
             return carry
 
-        lax.fori_loop(0, CZ, spread, 0)
+        lax.fori_loop(0, CZ, spread, 0, unroll=2)
     for k in range(ROUNDS):
         finish_send(k)
 
 
 def local(sizes, estimate, observed, psf_taps, view_shift, intersection):
     cz, cx, ny = estimate.shape
-    places = jnp.asarray(row_places())
+    turned = intersection.transpose(0, 2, 1)
     vmem = pl.BlockSpec(memory_space=pltpu.VMEM)
-    smem = pl.BlockSpec(memory_space=pltpu.SMEM)
+    hbm = pl.BlockSpec(memory_space=pltpu.HBM)
     dma = pltpu.SemaphoreType.DMA
     return pl.pallas_call(
         functools.partial(kernel, sizes),
         out_shape=jax.ShapeDtypeStruct((cz, cx, ny), F32),
-        in_specs=[smem, smem, smem, vmem, vmem, vmem],
+        in_specs=[hbm] * 5,
         out_specs=vmem,
         scratch_shapes=[
             pltpu.VMEM((16, ny // 128, 32, 128), F32),
@@ -328,12 +341,17 @@
             pltpu.VMEM((RANK, 16, 8, ny), F32),
             pltpu.VMEM((CZ, CX, ny), F32),
             pltpu.VMEM((CZ, CX, ny), F32),
-            dma((ROUNDS, 8)), dma((ROUNDS, 8)),
+            pltpu.SMEM(psf_taps.shape, F32),
+            pltpu.SMEM(view_shift.shape, jnp.int32),
+            pltpu.SMEM(turned.shape, jnp.int32),
+            pltpu.VMEM(estimate.shape, F32),
+            pltpu.VMEM(observed.shape, BF),
+            dma((ROUNDS, 8)), dma((ROUNDS, 8)), dma((5,)),
         ],
         compiler_params=pltpu.CompilerParams(
-            collective_id=0, has_side_effects=True, vmem_limit_bytes=24 * 1024 * 1024),
+            collective_id=0, has_side_effects=True, vmem_limit_bytes=56 * 1024 * 1024),
         cost_estimate=pl.CostEstimate(flops=10**9, bytes_accessed=10**6, transcendentals=5 * 10**6),
-    )(psf_taps, view_shift, intersection, estimate, observed, places)
+    )(psf_taps, view_shift, turned, estimate, observed)
 
 
 def solution(mesh):

time: 50.5 us -> 36 us (0.71)
  Pallas kernels: 45.3 us -> 34.2 us
  local copies, waits for them, and re-layouts: 4.86 us -> 1.67 us
    pallas_call x1, Pallas kernels: 45.3 us -> 34.2 us  [local(): pl.pallas_call(functools.partial(kernel, sizes), out_shape=jax.ShapeDtype...]
    unnamed x12 -> x1, local copies, waits for them, and re-layouts: 4.86 us -> 1.67 us
where the time goes in v3:
time: 36 us; the launch traced here: 35.9 us
  Pallas kernels  34.2 us (95%)
  local copies, waits for them, and re-layouts  1.67 us (5%)
    pallas_call x1, Pallas kernels, local(): pl.pallas_call(functools.partial(kernel, sizes), out_shape=jax.ShapeDtype...  34.2 us
    unnamed x1, local copies, waits for them, and re-layouts  1.67 us

profile of v3, /device:TPU:11, one launch (start us, length us, event | category | flops | bytes accessed | tf_op | source)
XLA Modules:
  0.0 35.9 jit_solution(3878910397474071260)
XLA Ops:
  0.0 34.2 %shard_map.55 = f32[8,16,512]{2,1,0:T(8,128)} custom-call(f32[3,3,3,9]{3,2,1,0:T(4,128)} %taps_in.1, s32[3]{0:T(128)} %shift_in.1, s32[3,4,8]{2,1,0:T(4,128)} %bitcast.1, f32[8,16,512]{2,1,0:T(8,128)} %est_in.1, bf16[3,8,16,512]{3,2,1,0:T(8,128)(2,1)} %obs_in.1), custom_call_target="tpu_custom_call" | custom-call | flops 1000000000 | bytes 1000000 | tf_op jit(solution)/shard_map/pallas_call | solution.py:325
  34.2 1.7 %copy.7 = f32[8,16,512]{2,1,0:T(8,128)} copy(f32[8,16,512]{2,1,0:T(8,128)} %shard_map.55) | data formatting | bytes 524288

commit v4 on v3

--- a/solution.py
+++ b/solution.py
@@ -12,6 +12,7 @@
 TAPS = 9
 PASSES = 8
 ROUNDS = 3 + VIEWS
+UNROLL = 8
 EPS_TV = 0.25
 TAU = 0.08
 BACKGROUND = 0.1
@@ -35,13 +36,13 @@
 
 def row_places():
     k = lax.broadcasted_iota(jnp.int32, (CZ + CX, FULL), 1)
-    z, x = k // CX, k % CX
+    z, x = k >> 4, k & (CX - 1)
     for (dz, dx), (first, rows) in SPOT.items():
         q = k - first
-        wide = CX if dx == 0 else RADIUS
+        bits = 4 if dx == 0 else 2
         here = (q >= 0) & (q < rows)
-        z = jnp.where(here, q // wide + (-RADIUS, 0, CZ)[dz + 1], z)
-        x = jnp.where(here, q % wide + (-RADIUS, 0, CX)[dx + 1], x)
+        z = jnp.where(here, (q >> bits) + (-RADIUS, 0, CZ)[dz + 1], z)
+        x = jnp.where(here, (q & ((1 << bits) - 1)) + (-RADIUS, 0, CX)[dx + 1], x)
     row = lax.broadcasted_iota(jnp.int32, (CZ + CX, FULL), 0)
     return jnp.where(row < CZ, z - row, x - row + CZ) + RADIUS
 
@@ -230,11 +231,11 @@
         def _():
             u[12] = u[11]
 
-        def planes(step, below):
-            z0 = p + step * (8 - p)
+        def planes(below):
+            z0 = p
             below = list(below)
             here = [u[z0, i] for i in range(3)]
-            for z in range(8 - p):
+            for z in range(16 - 2 * p):
                 after = [u[z0 + z + 1, i] for i in range(3)]
                 above = [flux(after[i] - here[i]) for i in range(3)]
                 fx = [flux(here[i + 1] - here[i]) * masks[i] for i in range(2)]
@@ -246,10 +247,9 @@
                     total = (above[i] - below[i]) + (fx[i] - fx_low[i]) + (fy - pltpu.roll(fy, 1, 1))
                     u[z0 + z, i] = here[i] + TAU * total
                 here, below = after, above
-            return tuple(below)
 
         first = tuple(flux(u[p, i] - u[p - 1, i]) for i in range(3))
-        lax.fori_loop(0, 2, planes, first)
+        planes(first)
 
     def natural(z, carry):
         for i in range(3):
@@ -270,7 +270,7 @@
     f2d = jnp.concatenate([fields[2], fields[2]], axis=0)
 
     def along_y(c, v, j, sign):
-        parts = [tmp[r, pl.ds(2 * j, 2)] for r in range(RANK)]
+        parts = [tmp[v % 2, r, pl.ds(2 * j, 2)] for r in range(RANK)]
         total = None
         for t in range(TAPS):
             term = c[v, t] * parts[0]
@@ -282,8 +282,13 @@
             total = term if total is None else total + term
         return total
 
+    def mix_planes(w, v, field):
+        tmp[v % 2] = jnp.dot(w[v], field, preferred_element_type=F32).reshape(tmp.shape[1:])
+
+    mix_planes(w_f, 0, f2d)
     for v in range(VIEWS):
-        tmp[...] = jnp.dot(w_f[v], f2d, preferred_element_type=F32).reshape(tmp.shape)
+        if v + 1 < VIEWS:
+            mix_planes(w_f, v + 1, f2d)
         flag = inter[v, ix, iz]
 
         def ratios(j, carry):
@@ -291,14 +296,14 @@
             img[j] = jnp.where(flag > 0, obs_r[v, j] / (image.reshape(CX, ny) + BACKGROUND), 1.0)
             return carry
 
-        lax.fori_loop(0, CZ, ratios, 0, unroll=2)
+        lax.fori_loop(0, CZ, ratios, 0, unroll=UNROLL)
         fill(3 + v, lambda z: img[z])
         start(3 + v)
 
     for v in range(VIEWS):
-        finish_recv(3 + v)
-        f3d = jnp.concatenate([fields[3 + v], fields[3 + v]], axis=0)
-        tmp[...] = jnp.dot(w_a[v], f3d, preferred_element_type=F32).reshape(tmp.shape)
+        for w in ((0, 1), (), (2,))[v]:
+            finish_recv(3 + w)
+            mix_planes(w_a, w, jnp.concatenate([fields[3 + w], fields[3 + w]], axis=0))
 
         def spread(j, carry):
             back = along_y(c_a, v, j, 1).reshape(CX, ny)
@@ -311,7 +316,7 @@
                 out[j] = smoothed * back / VIEWS
             return carry
 
-        lax.fori_loop(0, CZ, spread, 0, unroll=2)
+        lax.fori_loop(0, CZ, spread, 0, unroll=UNROLL)
     for k in range(ROUNDS):
         finish_send(k)
 
@@ -338,7 +343,7 @@
             pltpu.VMEM((VIEWS, RANK * TAPS, 8, ny), F32),
             pltpu.VMEM((VIEWS, RANK * TAPS, 8, ny), F32),
             pltpu.VMEM((VIEWS, cz, cx, ny), F32),
-            pltpu.VMEM((RANK, 16, 8, ny), F32),
+            pltpu.VMEM((2, RANK, 16, 8, ny), F32),
             pltpu.VMEM((CZ, CX, ny), F32),
             pltpu.VMEM((CZ, CX, ny), F32),
             pltpu.SMEM(psf_taps.shape, F32),

time: 36 us -> 42 us (1.17)
  Pallas kernels: 34.2 us -> 40.2 us
    pallas_call x1, Pallas kernels: 34.2 us -> 40.2 us  [local(): pl.pallas_call(functools.partial(kernel, sizes), out_shape=jax.ShapeDtype...]
where the time goes in v4:
time: 42 us; the launch traced here: 41.8 us
  Pallas kernels  40.2 us (96%)
  local copies, waits for them, and re-layouts  1.67 us (4%)
    pallas_call x1, Pallas kernels, local(): pl.pallas_call(functools.partial(kernel, sizes), out_shape=jax.ShapeDtype...  40.2 us
    unnamed x1, local copies, waits for them, and re-layouts  1.67 us

profile of v4, /device:TPU:11, one launch (start us, length us, event | category | flops | bytes accessed | tf_op | source)
XLA Modules:
  0.0 41.8 jit_solution(4519905320334845130)
XLA Ops:
  0.0 40.2 %shard_map.55 = f32[8,16,512]{2,1,0:T(8,128)} custom-call(f32[3,3,3,9]{3,2,1,0:T(4,128)} %taps_in.1, s32[3]{0:T(128)} %shift_in.1, s32[3,4,8]{2,1,0:T(4,128)} %bitcast.1, f32[8,16,512]{2,1,0:T(8,128)} %est_in.1, bf16[3,8,16,512]{3,2,1,0:T(8,128)(2,1)} %obs_in.1), custom_call_target="tpu_custom_call" | custom-call | flops 1000000000 | bytes 1000000 | tf_op jit(solution)/shard_map/pallas_call | solution.py:330
  40.2 1.7 %copy.7 = f32[8,16,512]{2,1,0:T(8,128)} copy(f32[8,16,512]{2,1,0:T(8,128)} %shard_map.55) | data formatting | bytes 524288

commit v5 on v3

--- a/solution.py
+++ b/solution.py
@@ -35,13 +35,13 @@
 
 def row_places():
     k = lax.broadcasted_iota(jnp.int32, (CZ + CX, FULL), 1)
-    z, x = k // CX, k % CX
+    z, x = k >> 4, k & (CX - 1)
     for (dz, dx), (first, rows) in SPOT.items():
         q = k - first
-        wide = CX if dx == 0 else RADIUS
+        bits = 4 if dx == 0 else 2
         here = (q >= 0) & (q < rows)
-        z = jnp.where(here, q // wide + (-RADIUS, 0, CZ)[dz + 1], z)
-        x = jnp.where(here, q % wide + (-RADIUS, 0, CX)[dx + 1], x)
+        z = jnp.where(here, (q >> bits) + (-RADIUS, 0, CZ)[dz + 1], z)
+        x = jnp.where(here, (q & ((1 << bits) - 1)) + (-RADIUS, 0, CX)[dx + 1], x)
     row = lax.broadcasted_iota(jnp.int32, (CZ + CX, FULL), 0)
     return jnp.where(row < CZ, z - row, x - row + CZ) + RADIUS
 
@@ -141,7 +141,6 @@
             def _():
                 copy_of(k, n).wait_recv()
 
-    start(0)
 
     lane = lax.broadcasted_iota(jnp.int32, (8, ny), 1)
     places = row_places()
@@ -182,11 +181,6 @@
         for z in range(CZ):
             obs_r[v, z] = pltpu.roll(obs[v, z].astype(F32), back, 1)
 
-    for load in loads[1:]:
-        load.wait()
-    prepare(0)
-    finish_recv(0)
-
     columns = range(ny // 128)
     for c in columns:
         nat[4:12, c, 8:24] = est[:, :, 128 * c:128 * c + 128]
@@ -257,17 +251,32 @@
                 nat[z, c, pl.ds(4 + i, 8, stride=3), :] = u[z, i, :, 128 * c:128 * c + 128]
         return carry
 
-    for half in range(2):
-        assemble(half)
-        for p in range(1, PASSES // 2 + 1):
-            tv(p)
-        lax.fori_loop(4, 12, natural, 0)
-        fill(half + 1, lambda z: jnp.concatenate([nat[4 + z, c, 8:24] for c in columns], axis=1))
-        start(half + 1)
-        prepare(half + 1)
-        finish_recv(half + 1)
-
-    f2d = jnp.concatenate([fields[2], fields[2]], axis=0)
+    def rim(k, carry):
+        start(k)
+
+        @pl.when(k == 0)
+        def _():
+            for load in loads[1:]:
+                load.wait()
+
+        prepare(k)
+        finish_recv(k)
+
+        @pl.when(k < 2)
+        def _():
+            assemble(k)
+            for p in range(1, PASSES // 2 + 1):
+                tv(p)
+            lax.fori_loop(4, 12, natural, 0)
+            fill(k + 1, lambda z: jnp.concatenate([nat[4 + z, c, 8:24] for c in columns], axis=1))
+
+        return carry
+
+    lax.fori_loop(0, 3, rim, 0)
+
+    def f2d(k):
+        field = fields[k]
+        return jnp.concatenate([field, field], axis=0)
 
     def along_y(c, v, j, sign):
         parts = [tmp[r, pl.ds(2 * j, 2)] for r in range(RANK)]
@@ -282,8 +291,8 @@
             total = term if total is None else total + term
         return total
 
-    for v in range(VIEWS):
-        tmp[...] = jnp.dot(w_f[v], f2d, preferred_element_type=F32).reshape(tmp.shape)
+    def forward(v, carry):
+        tmp[...] = jnp.dot(w_f[v], f2d(2), preferred_element_type=F32).reshape(tmp.shape)
         flag = inter[v, ix, iz]
 
         def ratios(j, carry):
@@ -294,26 +303,36 @@
         lax.fori_loop(0, CZ, ratios, 0, unroll=2)
         fill(3 + v, lambda z: img[z])
         start(3 + v)
-
-    for v in range(VIEWS):
+        return carry
+
+    lax.fori_loop(0, VIEWS, forward, 0)
+    corr[...] = jnp.zeros(corr.shape, F32)
+
+    def adjoint(v, carry):
         finish_recv(3 + v)
-        f3d = jnp.concatenate([fields[3 + v], fields[3 + v]], axis=0)
-        tmp[...] = jnp.dot(w_a[v], f3d, preferred_element_type=F32).reshape(tmp.shape)
+        tmp[...] = jnp.dot(w_a[v], f2d(3 + v), preferred_element_type=F32).reshape(tmp.shape)
 
         def spread(j, carry):
-            back = along_y(c_a, v, j, 1).reshape(CX, ny)
-            if v:
-                back = back + corr[j]
-            if v < VIEWS - 1:
-                corr[j] = back
-            else:
-                smoothed = jnp.concatenate([nat[4 + j, c, 8:24] for c in columns], axis=1)
-                out[j] = smoothed * back / VIEWS
+            corr[j] = corr[j] + along_y(c_a, v, j, 1).reshape(CX, ny)
             return carry
 
         lax.fori_loop(0, CZ, spread, 0, unroll=2)
-    for k in range(ROUNDS):
+        return carry
+
+    lax.fori_loop(0, VIEWS, adjoint, 0)
+
+    def finish(z, carry):
+        smoothed = jnp.concatenate([nat[4 + z, c, 8:24] for c in columns], axis=1)
+        out[z] = smoothed * corr[z] / VIEWS
+        return carry
+
+    lax.fori_loop(0, CZ, finish, 0)
+
+    def sent_all(k, carry):
         finish_send(k)
+        return carry
+
+    lax.fori_loop(0, ROUNDS, sent_all, 0)
 
 
 def local(sizes, estimate, observed, psf_taps, view_shift, intersection):

time: 36 us -> 36.1 us (level)
  no operation moved by 1% of the time
where the time goes in v5:
time: 36.1 us; the launch traced here: 35.9 us
  Pallas kernels  34.3 us (95%)
  local copies, waits for them, and re-layouts  1.67 us (5%)
    pallas_call x1, Pallas kernels, local(): pl.pallas_call(functools.partial(kernel, sizes), out_shape=jax.ShapeDtype...  34.3 us
    unnamed x1, local copies, waits for them, and re-layouts  1.67 us

profile of v5, /device:TPU:11, one launch (start us, length us, event | category | flops | bytes accessed | tf_op | source)
XLA Modules:
  0.0 35.9 jit_solution(10000537948501307391)
XLA Ops:
  0.0 34.3 %shard_map.55 = f32[8,16,512]{2,1,0:T(8,128)} custom-call(f32[3,3,3,9]{3,2,1,0:T(4,128)} %taps_in.1, s32[3]{0:T(128)} %shift_in.1, s32[3,4,8]{2,1,0:T(4,128)} %bitcast.1, f32[8,16,512]{2,1,0:T(8,128)} %est_in.1, bf16[3,8,16,512]{3,2,1,0:T(8,128)(2,1)} %obs_in.1), custom_call_target="tpu_custom_call" | custom-call | flops 1000000000 | bytes 1000000 | tf_op jit(solution)/shard_map/pallas_call | solution.py:344
  34.3 1.7 %copy.7 = f32[8,16,512]{2,1,0:T(8,128)} copy(f32[8,16,512]{2,1,0:T(8,128)} %shard_map.55) | data formatting | bytes 524288

commit v6 on v5

--- a/solution.py
+++ b/solution.py
@@ -205,7 +205,7 @@
                     u[z, i, :, 128 * c:128 * c + 128] = nat[z, c, pl.ds(4 + i, 8, stride=3), :]
             return carry
 
-        lax.fori_loop(0, 16, relayout, 0)
+        lax.fori_loop(0, 16, relayout, 0, unroll=4)
 
     sub = lax.broadcasted_iota(jnp.int32, (8, 128), 0)
     low_x = jnp.where(ix == 0, 0.0, 1.0)
@@ -267,7 +267,7 @@
             assemble(k)
             for p in range(1, PASSES // 2 + 1):
                 tv(p)
-            lax.fori_loop(4, 12, natural, 0)
+            lax.fori_loop(4, 12, natural, 0, unroll=4)
             fill(k + 1, lambda z: jnp.concatenate([nat[4 + z, c, 8:24] for c in columns], axis=1))
 
         return carry
@@ -326,7 +326,7 @@
         out[z] = smoothed * corr[z] / VIEWS
         return carry
 
-    lax.fori_loop(0, CZ, finish, 0)
+    lax.fori_loop(0, CZ, finish, 0, unroll=4)
 
     def sent_all(k, carry):
         finish_send(k)

time: 36.1 us -> 36 us (level)
  no operation moved by 1% of the time
where the time goes in v6:
time: 36 us; the launch traced here: 35.8 us
  Pallas kernels  34.1 us (95%)
  local copies, waits for them, and re-layouts  1.67 us (5%)
    pallas_call x1, Pallas kernels, local(): pl.pallas_call(functools.partial(kernel, sizes), out_shape=jax.ShapeDtype...  34.1 us
    unnamed x1, local copies, waits for them, and re-layouts  1.67 us

profile of v6, /device:TPU:11, one launch (start us, length us, event | category | flops | bytes accessed | tf_op | source)
XLA Modules:
  0.0 35.8 jit_solution(3377722433923207840)
XLA Ops:
  0.0 34.1 %shard_map.55 = f32[8,16,512]{2,1,0:T(8,128)} custom-call(f32[3,3,3,9]{3,2,1,0:T(4,128)} %taps_in.1, s32[3]{0:T(128)} %shift_in.1, s32[3,4,8]{2,1,0:T(4,128)} %bitcast.1, f32[8,16,512]{2,1,0:T(8,128)} %est_in.1, bf16[3,8,16,512]{3,2,1,0:T(8,128)(2,1)} %obs_in.1), custom_call_target="tpu_custom_call" | custom-call | flops 1000000000 | bytes 1000000 | tf_op jit(solution)/shard_map/pallas_call | solution.py:344
  34.1 1.7 %copy.7 = f32[8,16,512]{2,1,0:T(8,128)} copy(f32[8,16,512]{2,1,0:T(8,128)} %shard_map.55) | data formatting | bytes 524288
